TPU v7x, 32 devices: a whole 2x2x4 slice. The times are simulated.
32 devices in a mesh: row: 8 (over y, x, core), col: 4 (over z).
Axes of the slice: x: 2, y: 2, z: 4, core: 2. Of those that a mesh axis runs over, the one named last changes fastest.
Arguments:
- picture_encoder_output: bfloat16 [6144, 1152], P(('row', 'col')), may hold values from -0.59765625 to 0.59765625
- caption_encoder_output: bfloat16 [6144, 1152], P(('row', 'col')), may hold values from -0.59765625 to 0.59765625
- softness_factor_exponent: float32 [], replicated, may hold values from 2.7 to 3.7
- logit_offset_term: float32 [], replicated, may hold values from -5 to -2
Outputs:
- image_grad: float32 [6144, 1152], P(('row', 'col'))
- text_grad: float32 [6144, 1152], P(('row', 'col'))
All inputs are finite; a program needn't handle non-finite values.
Results may differ from a plain program's by a relative error of at most 0.008.
Values may be sent and summed in bfloat16 or wider, within the bound.
No kernel may reach another device: no remote copies, remote signals or barrier semaphores. Data moves between devices by JAX's collectives and lax.ppermute only.
A program may use at most 64 MiB of HBM per device.

v0:
```python
import functools

import jax
import jax.numpy as jnp
from jax import lax
from jax.experimental import pallas as pl
from jax.experimental.pallas import tpu as pltpu
from jax.sharding import PartitionSpec as P

eps_norm = 1e-06
VMEM = pl.BlockSpec(memory_space=pltpu.VMEM)
SMEM = pl.BlockSpec(memory_space=pltpu.SMEM)
HBM = pl.BlockSpec(memory_space=pltpu.HBM)
LIMIT = 24 * 2**20
PIECES = 4
CUTS = 2


def along(value, axis, target):
    count = lax.axis_size(axis)
    pairs = [(source, target(source) % count) for source in range(count)]
    return lax.ppermute(value, axis, pairs)


def inverse_norm(values):
    return lax.rsqrt(jnp.sum(values * values, axis=-1, keepdims=True) + eps_norm)


def unit_half(raw):
    values = raw.astype(jnp.float32)
    return (values * inverse_norm(values)).astype(jnp.bfloat16)


def weigh(own, other, scale_ref):
    scores = lax.dot_general(
        own, other, (((1,), (1,)), ((), ())), preferred_element_type=jnp.float32
    )
    return jax.nn.sigmoid(scale_ref[0:1, 0:1] * scores + scale_ref[1:2, 0:1])


def visit(own, other, scale_ref):
    weights = scale_ref[0:1, 0:1] * weigh(own, other, scale_ref)
    return jnp.dot(weights.astype(jnp.bfloat16), other, preferred_element_type=jnp.float32)


def odd_row():
    return lax.axis_index("row") & 1


def unit_back(raw, direction):
    values = raw.astype(jnp.float32)
    inverse = inverse_norm(values)
    unit = values * inverse
    share = jnp.sum(unit * direction, axis=-1, keepdims=True)
    return inverse * (direction - unit * share)


def pieces(rows, count=PIECES):
    if rows % (16 * count):
        return [(0, rows)]
    return [(n * rows // count, rows // count) for n in range(count)]


def cuts(block):
    return [
        jax.ShapeDtypeStruct((size,) + block.shape[1:], block.dtype)
        for _, size in pieces(block.shape[0], CUTS)
    ]


def call(kernel, out_shape, in_specs, out_specs, **more):
    return pl.pallas_call(
        kernel,
        out_shape=out_shape,
        in_specs=in_specs,
        out_specs=out_specs,
        compiler_params=pltpu.CompilerParams(vmem_limit_bytes=LIMIT),
        cost_estimate=pl.CostEstimate(flops=1000, bytes_accessed=1000, transcendentals=0),
        **more,
    )


def pick_kernel(img_ref, txt_ref, out_ref, sems):
    def copy(source):
        parts = [pl.ds(start, size) for start, size in pieces(out_ref.shape[0])]
        copies = [
            pltpu.make_async_copy(source.at[at], out_ref.at[at], sems.at[n])
            for n, at in enumerate(parts)
        ]
        for one in copies:
            one.start()
        for one in copies:
            one.wait()

    odd = odd_row()

    @pl.when(odd == 1)
    def _():
        copy(txt_ref)

    @pl.when(odd != 1)
    def _():
        copy(img_ref)


def pick(img, txt):
    return call(
        pick_kernel,
        jax.ShapeDtypeStruct(img.shape, img.dtype),
        [HBM, HBM],
        VMEM,
        scratch_shapes=[pltpu.SemaphoreType.DMA((len(pieces(img.shape[0])),))],
        name="pick",
    )(img, txt)


def load(sources, raw_refs, sems):
    parts = pieces(sources[0].shape[0])
    started = []
    for side, (source, raw_ref) in enumerate(zip(sources, raw_refs)):
        started.append([])
        for n, (start, size) in enumerate(parts):
            at = pl.ds(start, size)
            copy = pltpu.make_async_copy(source.at[at], raw_ref.at[at], sems.at[side, n])
            copy.start()
            started[-1].append((at, copy))
    return started


def norm_kernel(img_ref, txt_ref, img_half, txt_half, raw_ref, sems):
    halves = (img_half, txt_half)
    started = load((img_ref, txt_ref), (raw_ref.at[0], raw_ref.at[1]), sems)
    for side, copies in enumerate(started):
        for at, copy in copies:
            copy.wait()
            halves[side][at] = unit_half(raw_ref[side, at])


def norm(img, txt):
    rows, width = img.shape
    one = jax.ShapeDtypeStruct((rows, width), jnp.bfloat16)
    return call(
        norm_kernel,
        (one, one),
        [HBM, HBM],
        (VMEM, VMEM),
        scratch_shapes=[
            pltpu.VMEM((2, rows, width), jnp.bfloat16),
            pltpu.SemaphoreType.DMA((2, len(pieces(rows)))),
        ],
        name="norm",
    )(img, txt)


def own_kernel(
    exponent_ref, offset_ref, img_ref, txt_ref, img_half, txt_half,
    scale_ref, raw_ref, half_ref, near_ref, dir_ref, sems,
):
    started = load((img_ref, txt_ref), (raw_ref.at[0], raw_ref.at[1]), sems)
    scale_ref[0:1] = jnp.exp(jnp.broadcast_to(exponent_ref[...], (1, 128)))
    scale_ref[1:2] = jnp.broadcast_to(offset_ref[...], (1, 128))
    half_ref[0] = img_half[...]
    half_ref[1] = txt_half[...]
    near_ref[...] = half_ref[1 - odd_row()]
    img, txt = half_ref[0], half_ref[1]
    rows = img.shape[0]
    row = lax.broadcasted_iota(jnp.int32, (rows, rows), 0)
    column = lax.broadcasted_iota(jnp.int32, (rows, rows), 1)
    match = jnp.where(row == column, 1.0, 0.0)
    for side, (own, other) in enumerate(((img, txt), (txt, img))):
        weights = scale_ref[0:1, 0:1] * (weigh(own, other, scale_ref) - match)
        dir_ref[side] = jnp.dot(
            weights.astype(jnp.bfloat16), other, preferred_element_type=jnp.float32
        )
    for copies in started:
        for _, copy in copies:
            copy.wait()


def own_visit(exponent, offset, img, txt, img_half, txt_half):
    rows, width = img.shape
    both = jax.ShapeDtypeStruct((2, rows, width), jnp.bfloat16)
    return call(
        own_kernel,
        (
            jax.ShapeDtypeStruct((8, 128), jnp.float32),
            both,
            both,
            jax.ShapeDtypeStruct((rows, width), jnp.bfloat16),
            jax.ShapeDtypeStruct((2, rows, width), jnp.float32),
        ),
        [VMEM, VMEM, HBM, HBM, VMEM, VMEM],
        (VMEM,) * 5,
        scratch_shapes=[pltpu.SemaphoreType.DMA((2, len(pieces(rows))))],
        name="own",
    )(exponent.reshape(1, 1), offset.reshape(1, 1), img, txt, img_half, txt_half)


def parts_of(kinds, refs, rows):
    refs, blocks = list(refs), []
    for _ in kinds:
        block = [refs.pop(0)]
        while sum(part.shape[0] for part in block) < rows:
            block.append(refs.pop(0))
        blocks.append(block)
    return blocks


def flat(entries):
    kinds = tuple(kind for kind, _ in entries)
    return kinds, jax.tree.leaves([block for _, block in entries])


def visit_all(kinds, blocks, scale_ref, half_ref, dir_ref, acc_ref, others_ref):
    rows = half_ref.shape[1]
    blocks = parts_of(kinds, blocks, rows)
    held = [others_ref.at[pl.ds(n * rows, rows)] for n in range(len(kinds))]
    order = sorted(range(len(kinds)), key=lambda n: kinds[n][0])
    for place, n in enumerate(order):
        start = 0
        for part in blocks[n]:
            size = part.shape[0]
            block = part[...]
            held[place][pl.ds(start, size)] = unit_half(block) if kinds[n][1] else block
            start += size
    first = 0
    for side in (0, 1):
        count = sum(kind[0] == side for kind in kinds)
        if count:
            others = others_ref[pl.ds(first * rows, count * rows)]
            acc_ref[side] = dir_ref[side] + visit(half_ref[side], others, scale_ref)
        else:
            acc_ref[side] = dir_ref[side]
        first += count
    for place in range(first, len(kinds)):
        at = odd_row() if kinds[order[place]][0] == 2 else 1 - odd_row()
        acc_ref[at] += visit(half_ref[at], held[place][...], scale_ref)


def more_kernel(kinds, given, scale_ref, half_ref, dir_ref, *rest):
    blocks, rest = rest[: len(rest) - 2 - given], rest[len(rest) - 2 - given :]
    out_ref, halves, others_ref = rest[0], rest[1:-1], rest[-1]
    visit_all(kinds, blocks, scale_ref, half_ref, dir_ref, out_ref, others_ref)
    start = 0
    for cut in halves:
        cut[...] = others_ref[pl.ds(start, cut.shape[0])]
        start += cut.shape[0]


def finish(raw_ref, acc_ref, grad_ref, held_ref, sems):
    copies = []
    for n, (start, size) in enumerate(pieces(held_ref.shape[0])):
        at = pl.ds(start, size)
        held_ref[at] = unit_back(raw_ref[at], acc_ref[at])
        copies.append(pltpu.make_async_copy(held_ref.at[at], grad_ref.at[at], sems.at[n]))
        copies[-1].start()
    return copies


def last_kernel(kinds, scale_ref, half_ref, dir_ref, raw_ref, *rest):
    blocks, (img_grad, txt_grad, acc_ref, others_ref, held_ref, sems) = rest[:-6], rest[-6:]
    visit_all(kinds, blocks, scale_ref, half_ref, dir_ref, acc_ref, others_ref)
    copies = []
    for side, grad_ref in ((0, img_grad), (1, txt_grad)):
        copies += finish(
            raw_ref.at[side], acc_ref.at[side], grad_ref, held_ref.at[side], sems.at[side]
        )
    for copy in copies:
        copy.wait()


def more_visits(scale, half, direction, entries, give=False):
    kinds, blocks = flat(entries)
    rows, width = half.shape[1:]
    one = jax.ShapeDtypeStruct((rows, width), jnp.bfloat16)
    halves = cuts(one) * len(kinds) if give else []
    direction, *halves = call(
        functools.partial(more_kernel, kinds, len(halves)),
        (jax.ShapeDtypeStruct(direction.shape, direction.dtype), *halves),
        [VMEM] * (3 + len(blocks)),
        (VMEM,) * (1 + len(halves)),
        scratch_shapes=[pltpu.VMEM((len(kinds) * rows, width), jnp.bfloat16)],
        input_output_aliases={2: 0},
        name="more",
    )(scale, half, direction, *blocks)
    return (direction, halves) if give else direction


def unit_kernel(raw_ref, half_ref):
    half_ref[...] = unit_half(raw_ref[...])


def normalized(raw):
    return call(unit_kernel, jax.ShapeDtypeStruct(raw.shape, raw.dtype), [VMEM], VMEM, name="unit")(raw)


def last_visits(scale, half, direction, raw, entries):
    kinds, blocks = flat(entries)
    rows, width = half.shape[1:]
    grad = jax.ShapeDtypeStruct((rows, width), jnp.float32)
    return call(
        functools.partial(last_kernel, kinds),
        (grad, grad),
        [VMEM] * (4 + len(blocks)),
        (HBM, HBM),
        scratch_shapes=[
            pltpu.VMEM(direction.shape, direction.dtype),
            pltpu.VMEM((max(1, len(kinds)) * rows, width), jnp.bfloat16),
            pltpu.VMEM(direction.shape, direction.dtype),
            pltpu.SemaphoreType.DMA((2, len(pieces(rows)))),
        ],
        name="last",
    )(scale, half, direction, raw, *blocks)


def tied(entries, *others):
    blocks, others = lax.optimization_barrier(([block for _, block in entries], others))
    return [(kind, block) for (kind, _), block in zip(entries, blocks)], *others


def on_device(
    picture_encoder_output, caption_encoder_output, softness_factor_exponent, logit_offset_term
):
    img, txt = picture_encoder_output, caption_encoder_output
    row_extent = min(8, lax.axis_size("row") // 2)
    column_extent = min(4, lax.axis_size("col") // 2)
    paired = row_extent % 2 == 0 and lax.axis_size("row") % 2 == 0
    swap = lambda s: s ^ 1
    held = [pltpu.with_memory_space_constraint(a, pltpu.HBM) for a in (img, txt)]
    text_cols, image_cols, text_rows, image_rows, swapped, last = [], [], [], [], [], []
    for k in range(1, column_extent):
        text_cols.append(((0, True), along(txt, "col", lambda s: s + k)))
    img_half, txt_half = norm(*held)
    for k in range(1, column_extent):
        image_cols.append(((1, False), along(img_half, "col", lambda s: s - k)))
    scale, raw, half, near, direction = own_visit(
        softness_factor_exponent, logit_offset_term, *held, img_half, txt_half
    )
    if not paired:
        for k in range(1, row_extent):
            text_rows.append(((0, True), along(txt, "row", lambda s: s + k)))
            image_rows.append(((1, False), along(img_half, "row", lambda s: s - k)))
        last = text_cols + image_cols + text_rows + image_rows
        return last_visits(scale, half, direction, raw, last)

    reach = row_extent - 1
    far = along(pick(*held), "row", lambda s: s + reach if s % 2 else s - reach)
    for d in range(2, row_extent, 2):
        text_rows.append(((0, True), along(txt, "row", lambda s: s + d)))
        image_rows.append(((1, False), along(img_half, "row", lambda s: s - d)))
    if text_cols:
        direction = more_visits(scale, half, direction, text_cols)
    if text_rows:
        direction, halves = more_visits(scale, half, direction, text_rows, give=True)
        per = len(halves) // len(text_rows)
        for n in range(len(text_rows)):
            block = halves[n * per : (n + 1) * per]
            swapped.append(((0, False), [along(cut, "row", swap) for cut in block]))
        direction = more_visits(scale, half, direction, swapped)
    far, direction = lax.optimization_barrier((far, direction))
    middle = image_rows + image_cols + [((2, False), normalized(far))]
    middle, near, direction = tied(middle, near, direction)
    last = [(kind, along(block, "row", swap)) for kind, block in middle[: len(image_rows)]]
    last.append(((3, False), along(near, "row", swap)))
    direction = more_visits(scale, half, direction, middle)
    return last_visits(scale, half, direction, raw, last)


def solution(mesh):
    return jax.shard_map(
        on_device,
        mesh=mesh,
        in_specs=(P(("row", "col"), None), P(("row", "col"), None), P(), P()),
        out_specs=(P(("row", "col"), None), P(("row", "col"), None)),
        check_vma=False,
    )
```

profile of v0, /device:TPU:19, one launch (start us, length us, event | category | flops | bytes accessed | tf_op | source)
XLA Modules:
  0.0 33.0 jit_solution(14834103963042560847)
XLA Ops:
  0.6 1.3 %collective-permute-start.3 = (bf16[192,1152]{1,0:T(8,128)(2,1)}, bf16[192,1152]{1,0:T(8,128)(2,1)S(1)}, u32[]{:S(2)}, u32[]{:S(2)}) collective-permute-start(bf16[192,1152]{1,0:T(8,128)(2,1)} %txt_ref.5), channel_id=1, source_target_pairs={{0,1},{1,2},{2,3},{3,0},{4,5},{5,6},{6,7},{7,4},{8,9},{9,10},{10,1... | collective-permute-start | bytes 1327112 | tf_op jit(solution)/shard_map/ppermute | solution.py:22
  2.0 1.2 %collective-permute-start.4 = (bf16[192,1152]{1,0:T(8,128)(2,1)}, bf16[192,1152]{1,0:T(8,128)(2,1)S(1)}, u32[]{:S(2)}, u32[]{:S(2)}) collective-permute-start(bf16[192,1152]{1,0:T(8,128)(2,1)} %txt_ref.5), channel_id=1, source_target_pairs={{0,8},{4,12},{8,16},{12,20},{16,24},{20,28},{24,0},{28,4},{1,9},{5... | collective-permute-start | bytes 1327112 | tf_op jit(solution)/shard_map/ppermute | solution.py:22
  3.2 1.1 %pick.1 = bf16[192,1152]{1,0:T(8,128)(2,1)S(1)} custom-call(bf16[192,1152]{1,0:T(8,128)(2,1)} %img_ref.5, bf16[192,1152]{1,0:T(8,128)(2,1)} %txt_ref.5), custom_call_target="tpu_custom_call" | custom-call | flops 1000 | bytes 1000 | tf_op jit(solution)/shard_map/pick/pallas_call | solution.py:107
  4.3 1.4 %collective-permute-start.2 = (bf16[192,1152]{1,0:T(8,128)(2,1)S(1)}, bf16[192,1152]{1,0:T(8,128)(2,1)S(1)}, u32[]{:S(2)}, u32[]{:S(2)}) collective-permute-start(bf16[192,1152]{1,0:T(8,128)(2,1)S(1)} %pick.1), channel_id=1, source_target_pairs={{0,20},{4,16},{8,28},{12,24},{16,4},{20,0},{24,12},{28,8},{1,21},{... | collective-permute-start | bytes 1327112 | tf_op jit(solution)/shard_map/ppermute | solution.py:22
  5.7 1.9 %norm.1 = (bf16[192,1152]{1,0:T(8,128)(2,1)S(1)}, bf16[192,1152]{1,0:T(8,128)(2,1)S(1)}) custom-call(bf16[192,1152]{1,0:T(8,128)(2,1)} %img_ref.5, bf16[192,1152]{1,0:T(8,128)(2,1)} %txt_ref.5), custom_call_target="tpu_custom_call" | custom-call | flops 1000 | bytes 1000 | tf_op jit(solution)/shard_map/norm/pallas_call | solution.py:142
  7.6 1.3 %collective-permute-start = (bf16[192,1152]{1,0:T(8,128)(2,1)S(1)}, bf16[192,1152]{1,0:T(8,128)(2,1)S(1)}, u32[]{:S(2)}, u32[]{:S(2)}) collective-permute-start(bf16[192,1152]{1,0:T(8,128)(2,1)S(1)} %get-tuple-element.19.img_half), channel_id=1, source_target_pairs={{0,24},{4,28},{8,0},{12,4},{16,8},{20,12},{24,16},{28,20},{1,25},{... | collective-permute-start | bytes 1327112 | tf_op jit(solution)/shard_map/ppermute | solution.py:22
  8.9 0.2 collective-permute-start.1
  10.4 2.3 %own.1 = (f32[8,128]{1,0:T(8,128)S(1)}, bf16[2,192,1152]{2,1,0:T(8,128)(2,1)S(1)}, bf16[2,192,1152]{2,1,0:T(8,128)(2,1)S(1)}, bf16[192,1152]{1,0:T(8,128)(2,1)S(1)}, f32[2,192,1152]{2,1,0:T(8,128)S(1)}) custom-call(f32[1,1]{1,0:T(1,128)} %bitcast.2.exponent_ref, f32[1,1]{1,0:T(1,128)} %bitcast.3.offset_ref, bf16[192,1152]{1,0:T(8,128)(2,1)} %img_ref.5, ...), custom_call_target="tpu_custom_call" | custom-call | flops 1000 | bytes 1000 | tf_op jit(solution)/shard_map/own/pallas_call | solution.py:183
  12.7 1.0 %more.4.dir_ref = f32[2,192,1152]{2,1,0:T(8,128)S(1)} custom-call(f32[8,128]{1,0:T(8,128)S(1)} %get-tuple-element.21.scale_ref, bf16[2,192,1152]{2,1,0:T(8,128)(2,1)S(1)} %get-tuple-element.22.half_ref, f32[2,192,1152]{2,1,0:T(8,128)S(1)} %get-tuple-element.23.dir_ref, ...), custom_call_target="tpu_custom_call", output_to_operand_aliasing={{}: (2, {})} | custom-call | flops 1000 | bytes 1000 | tf_op jit(solution)/shard_map/more/pallas_call | solution.py:277
  13.6 0.0 collective-permute-done.4.rest_0_
  13.7 1.0 %more.5 = (f32[2,192,1152]{2,1,0:T(8,128)S(1)}, bf16[96,1152]{1,0:T(8,128)(2,1)S(1)}, bf16[96,1152]{1,0:T(8,128)(2,1)S(1)}) custom-call(f32[8,128]{1,0:T(8,128)S(1)} %get-tuple-element.21.scale_ref, bf16[2,192,1152]{2,1,0:T(8,128)(2,1)S(1)} %get-tuple-element.22.half_ref, f32[2,192,1152]{2,1,0:T(8,128)S(1)} %more.4.dir_ref, ...), custom_call_target="tpu_custom_call", output_to_operand_aliasing={{0}: (2, {})} | custom-call | flops 1000 | bytes 1000 | tf_op jit(solution)/shard_map/more/pallas_call | solution.py:277
  14.6 10.4 %collective-permute-start.5 = (bf16[96,1152]{1,0:T(8,128)(2,1)S(1)}, bf16[96,1152]{1,0:T(8,128)(2,1)S(1)}, u32[]{:S(2)}, u32[]{:S(2)}) collective-permute-start(bf16[96,1152]{1,0:T(8,128)(2,1)S(1)} %get-tuple-element.25), channel_id=1, source_target_pairs={{0,4},{4,0},{8,12},{12,8},{16,20},{20,16},{24,28},{28,24},{1,5},{5... | collective-permute-start | bytes 663560 | tf_op jit(solution)/shard_map/ppermute | solution.py:22
  25.0 0.1 collective-permute-start.6
  25.1 1.0 %collective-permute-done.5.rest_0_ = bf16[96,1152]{1,0:T(8,128)(2,1)S(1)} collective-permute-done((bf16[96,1152]{1,0:T(8,128)(2,1)S(1)}, bf16[96,1152]{1,0:T(8,128)(2,1)S(1)}, u32[]{:S(2)}, u32[]{:S(2)}) %collective-permute-start.5) | collective-permute-done | bytes 221216 | tf_op jit(solution)/shard_map/ppermute | solution.py:22
  26.1 0.4 %collective-permute-done.6.rest_1_ = bf16[96,1152]{1,0:T(8,128)(2,1)S(1)} collective-permute-done((bf16[96,1152]{1,0:T(8,128)(2,1)S(1)}, bf16[96,1152]{1,0:T(8,128)(2,1)S(1)}, u32[]{:S(2)}, u32[]{:S(2)}) %collective-permute-start.6) | collective-permute-done | bytes 221216 | tf_op jit(solution)/shard_map/ppermute | solution.py:22
  26.5 0.8 %more.6.dir_ref = f32[2,192,1152]{2,1,0:T(8,128)S(1)} custom-call(f32[8,128]{1,0:T(8,128)S(1)} %get-tuple-element.21.scale_ref, bf16[2,192,1152]{2,1,0:T(8,128)(2,1)S(1)} %get-tuple-element.22.half_ref, f32[2,192,1152]{2,1,0:T(8,128)S(1)} %get-tuple-element.24.dir_ref, ...), custom_call_target="tpu_custom_call", output_to_operand_aliasing={{}: (2, {})} | custom-call | flops 1000 | bytes 1000 | tf_op jit(solution)/shard_map/more/pallas_call | solution.py:277
  27.3 0.0 collective-permute-done.2.raw_ref
  27.3 0.2 unit.1.rest_2_
  27.5 0.0 collective-permute-done.rest_0_
  27.5 0.4 %collective-permute-start.7 = (bf16[192,1152]{1,0:T(8,128)(2,1)S(1)}, bf16[192,1152]{1,0:T(8,128)(2,1)S(1)}, u32[]{:S(2)}, u32[]{:S(2)}) collective-permute-start(bf16[192,1152]{1,0:T(8,128)(2,1)S(1)} %collective-permute-done.rest_0_), channel_id=1, source_target_pairs={{0,4},{4,0},{8,12},{12,8},{16,20},{20,16},{24,28},{28,24},{1,5},{5... | collective-permute-start | bytes 1327112 | tf_op jit(solution)/shard_map/ppermute | solution.py:22
  27.9 0.2 collective-permute-start.8
  28.1 1.7 %more.7.dir_ref = f32[2,192,1152]{2,1,0:T(8,128)S(1)} custom-call(f32[8,128]{1,0:T(8,128)S(1)} %get-tuple-element.21.scale_ref, bf16[2,192,1152]{2,1,0:T(8,128)(2,1)S(1)} %get-tuple-element.22.half_ref, f32[2,192,1152]{2,1,0:T(8,128)S(1)} %more.6.dir_ref, bf16[192,1152]{1,0:T(8,128)(2,1)S(1)} %collective-permute-done.rest_0_, ...), custom_call_target="tpu_custom_call", output_to_operand_aliasing={{}: (2, {})} | custom-call | flops 1000 | bytes 1000 | tf_op jit(solution)/shard_map/more/pallas_call | solution.py:277
  29.8 0.2 collective-permute-done.8.rest_1_
  30.0 3.0 %last.1 = (f32[192,1152]{1,0:T(8,128)}, f32[192,1152]{1,0:T(8,128)}) custom-call(f32[8,128]{1,0:T(8,128)S(1)} %get-tuple-element.21.scale_ref, bf16[2,192,1152]{2,1,0:T(8,128)(2,1)S(1)} %get-tuple-element.22.half_ref, f32[2,192,1152]{2,1,0:T(8,128)S(1)} %more.7.dir_ref, bf16[2,192,1152]{2,1,0:T(8,128)(2,1)S(1)} %get-tuple-element.34.raw_ref, ...), custom_call_target="tpu_custom_call" | custom-call | flops 1000 | bytes 1000 | tf_op jit(solution)/shard_map/last/pallas_call | solution.py:301
  (3 shorter events, 0.0 us)
Async XLA Ops:
  0.6 12.0 %collective-permute-start.3 = (bf16[192,1152]{1,0:T(8,128)(2,1)}, bf16[192,1152]{1,0:T(8,128)(2,1)S(1)}, u32[]{:S(2)}, u32[]{:S(2)}) collective-permute-start(bf16[192,1152]{1,0:T(8,128)(2,1)} %txt_ref.5), channel_id=1, source_target_pairs={{0,1},{1,2},{2,3},{3,0},{4,5},{5,6},{6,7},{7,4},{8,9},{9,10},{10,1... | collective-permute-start | bytes 1327112 | tf_op jit(solution)/shard_map/ppermute | solution.py:22
  2.0 11.7 %collective-permute-start.4 = (bf16[192,1152]{1,0:T(8,128)(2,1)}, bf16[192,1152]{1,0:T(8,128)(2,1)S(1)}, u32[]{:S(2)}, u32[]{:S(2)}) collective-permute-start(bf16[192,1152]{1,0:T(8,128)(2,1)} %txt_ref.5), channel_id=1, source_target_pairs={{0,8},{4,12},{8,16},{12,20},{16,24},{20,28},{24,0},{28,4},{1,9},{5... | collective-permute-start | bytes 1327112 | tf_op jit(solution)/shard_map/ppermute | solution.py:22
  4.3 23.0 %collective-permute-start.2 = (bf16[192,1152]{1,0:T(8,128)(2,1)S(1)}, bf16[192,1152]{1,0:T(8,128)(2,1)S(1)}, u32[]{:S(2)}, u32[]{:S(2)}) collective-permute-start(bf16[192,1152]{1,0:T(8,128)(2,1)S(1)} %pick.1), channel_id=1, source_target_pairs={{0,20},{4,16},{8,28},{12,24},{16,4},{20,0},{24,12},{28,8},{1,21},{... | collective-permute-start | bytes 1327112 | tf_op jit(solution)/shard_map/ppermute | solution.py:22
  7.6 19.9 %collective-permute-start = (bf16[192,1152]{1,0:T(8,128)(2,1)S(1)}, bf16[192,1152]{1,0:T(8,128)(2,1)S(1)}, u32[]{:S(2)}, u32[]{:S(2)}) collective-permute-start(bf16[192,1152]{1,0:T(8,128)(2,1)S(1)} %get-tuple-element.19.img_half), channel_id=1, source_target_pairs={{0,24},{4,28},{8,0},{12,4},{16,8},{20,12},{24,16},{28,20},{1,25},{... | collective-permute-start | bytes 1327112 | tf_op jit(solution)/shard_map/ppermute | solution.py:22
  8.9 18.6 %collective-permute-start.1 = (bf16[192,1152]{1,0:T(8,128)(2,1)S(1)}, bf16[192,1152]{1,0:T(8,128)(2,1)S(1)}, u32[]{:S(2)}, u32[]{:S(2)}) collective-permute-start(bf16[192,1152]{1,0:T(8,128)(2,1)S(1)} %get-tuple-element.19.img_half), channel_id=1, source_target_pairs={{0,3},{1,0},{2,1},{3,2},{4,7},{5,4},{6,5},{7,6},{8,11},{9,8},{10,9... | collective-permute-start | bytes 1327112 | tf_op jit(solution)/shard_map/ppermute | solution.py:22
  14.6 11.5 %collective-permute-start.5 = (bf16[96,1152]{1,0:T(8,128)(2,1)S(1)}, bf16[96,1152]{1,0:T(8,128)(2,1)S(1)}, u32[]{:S(2)}, u32[]{:S(2)}) collective-permute-start(bf16[96,1152]{1,0:T(8,128)(2,1)S(1)} %get-tuple-element.25), channel_id=1, source_target_pairs={{0,4},{4,0},{8,12},{12,8},{16,20},{20,16},{24,28},{28,24},{1,5},{5... | collective-permute-start | bytes 663560 | tf_op jit(solution)/shard_map/ppermute | solution.py:22
  25.0 1.5 %collective-permute-start.6 = (bf16[96,1152]{1,0:T(8,128)(2,1)S(1)}, bf16[96,1152]{1,0:T(8,128)(2,1)S(1)}, u32[]{:S(2)}, u32[]{:S(2)}) collective-permute-start(bf16[96,1152]{1,0:T(8,128)(2,1)S(1)} %get-tuple-element.26), channel_id=1, source_target_pairs={{0,4},{4,0},{8,12},{12,8},{16,20},{20,16},{24,28},{28,24},{1,5},{5... | collective-permute-start | bytes 663560 | tf_op jit(solution)/shard_map/ppermute | solution.py:22
  27.5 2.3 %collective-permute-start.7 = (bf16[192,1152]{1,0:T(8,128)(2,1)S(1)}, bf16[192,1152]{1,0:T(8,128)(2,1)S(1)}, u32[]{:S(2)}, u32[]{:S(2)}) collective-permute-start(bf16[192,1152]{1,0:T(8,128)(2,1)S(1)} %collective-permute-done.rest_0_), channel_id=1, source_target_pairs={{0,4},{4,0},{8,12},{12,8},{16,20},{20,16},{24,28},{28,24},{1,5},{5... | collective-permute-start | bytes 1327112 | tf_op jit(solution)/shard_map/ppermute | solution.py:22
  27.9 2.1 %collective-permute-start.8 = (bf16[192,1152]{1,0:T(8,128)(2,1)S(1)}, bf16[192,1152]{1,0:T(8,128)(2,1)S(1)}, u32[]{:S(2)}, u32[]{:S(2)}) collective-permute-start(bf16[192,1152]{1,0:T(8,128)(2,1)S(1)} %get-tuple-element.35), channel_id=1, source_target_pairs={{0,4},{4,0},{8,12},{12,8},{16,20},{20,16},{24,28},{28,24},{1,5},{5... | collective-permute-start | bytes 1327112 | tf_op jit(solution)/shard_map/ppermute | solution.py:22
where the time goes:
time: 33.2 us; the launch traced here: 33 us
  starting transfers between devices  16.5 us (50%)
  Pallas kernels  12.9 us (39%)
  between operations  2.03 us (6%)
  waiting for transfers between devices  1.64 us (5%)
    ppermute x9, starting transfers between devices, along(): return lax.ppermute(value, axis, pairs)  16.5 us
    pallas_call x4, Pallas kernels, more_visits(): call(functools.partial(more_kernel, kinds, len(halves)), (jax.ShapeDtypeS...  4.48 us
    pallas_call x1, Pallas kernels, last_visits(): call(functools.partial(last_kernel, kinds), (grad, grad), [VMEM] * (4 + l...  2.96 us
    pallas_call x1, Pallas kernels, own_visit(): call(own_kernel, (jax.ShapeDtypeStruct((8, 128), jnp.float32), both, both...  2.27 us
    pallas_call x1, Pallas kernels, norm(): call(norm_kernel, (one, one), [HBM, HBM], (VMEM, VMEM), scratch_shapes=[p...  1.87 us
    ppermute x9, waiting for transfers between devices, along(): return lax.ppermute(value, axis, pairs)  1.64 us
    pallas_call x1, Pallas kernels, pick(): call(pick_kernel, jax.ShapeDtypeStruct(img.shape, img.dtype), [HBM, HBM],...  1.09 us
  transfers between devices with their start and end apart: 9, of which 3 were waited for; matrix products, arithmetic and copies ran while one was open for 0% of the time, Pallas kernels for 30%

commit v1 on v0

--- a/solution.py
+++ b/solution.py
@@ -211,7 +211,7 @@
     return kinds, jax.tree.leaves([block for _, block in entries])
 
 
-def visit_all(kinds, blocks, scale_ref, half_ref, dir_ref, acc_ref, others_ref):
+def visit_all(kinds, blocks, scale_ref, half_ref, dir_ref, acc_ref, others_ref, sides=(0, 1)):
     rows = half_ref.shape[1]
     blocks = parts_of(kinds, blocks, rows)
     held = [others_ref.at[pl.ds(n * rows, rows)] for n in range(len(kinds))]
@@ -224,7 +224,7 @@
             held[place][pl.ds(start, size)] = unit_half(block) if kinds[n][1] else block
             start += size
     first = 0
-    for side in (0, 1):
+    for side in sides:
         count = sum(kind[0] == side for kind in kinds)
         if count:
             others = others_ref[pl.ds(first * rows, count * rows)]
@@ -259,12 +259,17 @@
 
 def last_kernel(kinds, scale_ref, half_ref, dir_ref, raw_ref, *rest):
     blocks, (img_grad, txt_grad, acc_ref, others_ref, held_ref, sems) = rest[:-6], rest[-6:]
-    visit_all(kinds, blocks, scale_ref, half_ref, dir_ref, acc_ref, others_ref)
-    copies = []
-    for side, grad_ref in ((0, img_grad), (1, txt_grad)):
+    texts = [n for n, (side, _) in enumerate(kinds) if side == 1]
+    late = [(kinds[n], blocks[n]) for n in texts]
+    early = [(kinds[n], blocks[n]) for n in range(len(kinds)) if n not in texts]
+    copies, source = [], dir_ref
+    for side, entries, grad_ref in ((0, early, img_grad), (1, late, txt_grad)):
+        sides = (0, 1) if side == 0 else (1,)
+        visit_all(*flat(entries), scale_ref, half_ref, source, acc_ref, others_ref, sides)
         copies += finish(
             raw_ref.at[side], acc_ref.at[side], grad_ref, held_ref.at[side], sems.at[side]
         )
+        source = acc_ref
     for copy in copies:
         copy.wait()
 
@@ -348,15 +353,14 @@
     for d in range(2, row_extent, 2):
         text_rows.append(((0, True), along(txt, "row", lambda s: s + d)))
         image_rows.append(((1, False), along(img_half, "row", lambda s: s - d)))
-    if text_cols:
-        direction = more_visits(scale, half, direction, text_cols)
     if text_rows:
         direction, halves = more_visits(scale, half, direction, text_rows, give=True)
         per = len(halves) // len(text_rows)
         for n in range(len(text_rows)):
             block = halves[n * per : (n + 1) * per]
             swapped.append(((0, False), [along(cut, "row", swap) for cut in block]))
-        direction = more_visits(scale, half, direction, swapped)
+    if text_cols + swapped:
+        direction = more_visits(scale, half, direction, text_cols + swapped)
     far, direction = lax.optimization_barrier((far, direction))
     middle = image_rows + image_cols + [((2, False), normalized(far))]
     middle, near, direction = tied(middle, near, direction)

time: 33.2 us -> 32.2 us (0.970)
  Pallas kernels: 12.9 us -> 11.8 us
    pallas_call x4 -> x3, Pallas kernels: 4.48 us -> 3.77 us  [more_visits(): call(functools.partial(more_kernel, kinds, len(halves)), (jax.ShapeDtypeS...]
  transfers between devices with their start and end apart: 9 -> 9, of which waited for: 3 -> 2; matrix products, arithmetic and copies ran while one was open for 0% -> 0% of each run, Pallas kernels for 30% -> 29%
where the time goes in v1:
time: 32.2 us; the launch traced here: 32 us
  starting transfers between devices  16.7 us (52%)
  Pallas kernels  11.8 us (37%)
  between operations  2.02 us (6%)
  waiting for transfers between devices  1.41 us (4%)
    ppermute x9, starting transfers between devices, along(): return lax.ppermute(value, axis, pairs)  16.7 us
    pallas_call x3, Pallas kernels, more_visits(): call(functools.partial(more_kernel, kinds, len(halves)), (jax.ShapeDtypeS...  3.77 us
    pallas_call x1, Pallas kernels, last_visits(): call(functools.partial(last_kernel, kinds), (grad, grad), [VMEM] * (4 + l...  2.66 us
    pallas_call x1, Pallas kernels, own_visit(): call(own_kernel, (jax.ShapeDtypeStruct((8, 128), jnp.float32), both, both...  2.27 us
    pallas_call x1, Pallas kernels, norm(): call(norm_kernel, (one, one), [HBM, HBM], (VMEM, VMEM), scratch_shapes=[p...  1.87 us
    ppermute x9, waiting for transfers between devices, along(): return lax.ppermute(value, axis, pairs)  1.41 us
    pallas_call x1, Pallas kernels, pick(): call(pick_kernel, jax.ShapeDtypeStruct(img.shape, img.dtype), [HBM, HBM],...  1.09 us
  transfers between devices with their start and end apart: 9, of which 2 were waited for; matrix products, arithmetic and copies ran while one was open for 0% of the time, Pallas kernels for 29%

profile of v1, /device:TPU:19, one launch (start us, length us, event | category | flops | bytes accessed | tf_op | source)
XLA Modules:
  0.0 32.0 jit_solution(14913208328873085302)
XLA Ops:
  0.6 1.3 %collective-permute-start.3 = (bf16[192,1152]{1,0:T(8,128)(2,1)}, bf16[192,1152]{1,0:T(8,128)(2,1)S(1)}, u32[]{:S(2)}, u32[]{:S(2)}) collective-permute-start(bf16[192,1152]{1,0:T(8,128)(2,1)} %txt_ref.5), channel_id=1, source_target_pairs={{0,8},{4,12},{8,16},{12,20},{16,24},{20,28},{24,0},{28,4},{1,9},{5... | collective-permute-start | bytes 1327112 | tf_op jit(solution)/shard_map/ppermute | solution.py:22
  1.9 1.3 %collective-permute-start.4 = (bf16[192,1152]{1,0:T(8,128)(2,1)}, bf16[192,1152]{1,0:T(8,128)(2,1)S(1)}, u32[]{:S(2)}, u32[]{:S(2)}) collective-permute-start(bf16[192,1152]{1,0:T(8,128)(2,1)} %txt_ref.5), channel_id=1, source_target_pairs={{0,1},{1,2},{2,3},{3,0},{4,5},{5,6},{6,7},{7,4},{8,9},{9,10},{10,1... | collective-permute-start | bytes 1327112 | tf_op jit(solution)/shard_map/ppermute | solution.py:22
  3.2 1.1 %pick.1 = bf16[192,1152]{1,0:T(8,128)(2,1)S(1)} custom-call(bf16[192,1152]{1,0:T(8,128)(2,1)} %img_ref.5, bf16[192,1152]{1,0:T(8,128)(2,1)} %txt_ref.5), custom_call_target="tpu_custom_call" | custom-call | flops 1000 | bytes 1000 | tf_op jit(solution)/shard_map/pick/pallas_call | solution.py:107
  4.3 1.4 %collective-permute-start.2 = (bf16[192,1152]{1,0:T(8,128)(2,1)S(1)}, bf16[192,1152]{1,0:T(8,128)(2,1)S(1)}, u32[]{:S(2)}, u32[]{:S(2)}) collective-permute-start(bf16[192,1152]{1,0:T(8,128)(2,1)S(1)} %pick.1), channel_id=1, source_target_pairs={{0,20},{4,16},{8,28},{12,24},{16,4},{20,0},{24,12},{28,8},{1,21},{... | collective-permute-start | bytes 1327112 | tf_op jit(solution)/shard_map/ppermute | solution.py:22
  5.7 1.9 %norm.1 = (bf16[192,1152]{1,0:T(8,128)(2,1)S(1)}, bf16[192,1152]{1,0:T(8,128)(2,1)S(1)}) custom-call(bf16[192,1152]{1,0:T(8,128)(2,1)} %img_ref.5, bf16[192,1152]{1,0:T(8,128)(2,1)} %txt_ref.5), custom_call_target="tpu_custom_call" | custom-call | flops 1000 | bytes 1000 | tf_op jit(solution)/shard_map/norm/pallas_call | solution.py:142
  7.6 1.3 %collective-permute-start = (bf16[192,1152]{1,0:T(8,128)(2,1)S(1)}, bf16[192,1152]{1,0:T(8,128)(2,1)S(1)}, u32[]{:S(2)}, u32[]{:S(2)}) collective-permute-start(bf16[192,1152]{1,0:T(8,128)(2,1)S(1)} %get-tuple-element.19.img_half), channel_id=1, source_target_pairs={{0,24},{4,28},{8,0},{12,4},{16,8},{20,12},{24,16},{28,20},{1,25},{... | collective-permute-start | bytes 1327112 | tf_op jit(solution)/shard_map/ppermute | solution.py:22
  8.9 0.2 collective-permute-start.1
  10.4 2.3 %own.1 = (f32[8,128]{1,0:T(8,128)S(1)}, bf16[2,192,1152]{2,1,0:T(8,128)(2,1)S(1)}, bf16[2,192,1152]{2,1,0:T(8,128)(2,1)S(1)}, bf16[192,1152]{1,0:T(8,128)(2,1)S(1)}, f32[2,192,1152]{2,1,0:T(8,128)S(1)}) custom-call(f32[1,1]{1,0:T(1,128)} %bitcast.2.exponent_ref, f32[1,1]{1,0:T(1,128)} %bitcast.3.offset_ref, bf16[192,1152]{1,0:T(8,128)(2,1)} %img_ref.5, ...), custom_call_target="tpu_custom_call" | custom-call | flops 1000 | bytes 1000 | tf_op jit(solution)/shard_map/own/pallas_call | solution.py:183
  12.7 1.0 %more.3 = (f32[2,192,1152]{2,1,0:T(8,128)S(1)}, bf16[96,1152]{1,0:T(8,128)(2,1)S(1)}, bf16[96,1152]{1,0:T(8,128)(2,1)S(1)}) custom-call(f32[8,128]{1,0:T(8,128)S(1)} %get-tuple-element.21.scale_ref, bf16[2,192,1152]{2,1,0:T(8,128)(2,1)S(1)} %get-tuple-element.22.half_ref, ...), custom_call_target="tpu_custom_call", output_to_operand_aliasing={{0}: (2, {})} | custom-call | flops 1000 | bytes 1000 | tf_op jit(solution)/shard_map/more/pallas_call | solution.py:282
  13.7 2.0 %collective-permute-start.5 = (bf16[96,1152]{1,0:T(8,128)(2,1)S(1)}, bf16[96,1152]{1,0:T(8,128)(2,1)S(1)}, u32[]{:S(2)}, u32[]{:S(2)}) collective-permute-start(bf16[96,1152]{1,0:T(8,128)(2,1)S(1)} %get-tuple-element.25), channel_id=1, source_target_pairs={{0,4},{4,0},{8,12},{12,8},{16,20},{20,16},{24,28},{28,24},{1,5},{5... | collective-permute-start | bytes 663560 | tf_op jit(solution)/shard_map/ppermute | solution.py:22
  15.7 0.0 collective-permute-done.4.rest_0_
  15.7 8.5 %collective-permute-start.6 = (bf16[96,1152]{1,0:T(8,128)(2,1)S(1)}, bf16[96,1152]{1,0:T(8,128)(2,1)S(1)}, u32[]{:S(2)}, u32[]{:S(2)}) collective-permute-start(bf16[96,1152]{1,0:T(8,128)(2,1)S(1)} %get-tuple-element.26), channel_id=1, source_target_pairs={{0,4},{4,0},{8,12},{12,8},{16,20},{20,16},{24,28},{28,24},{1,5},{5... | collective-permute-start | bytes 663560 | tf_op jit(solution)/shard_map/ppermute | solution.py:22
  24.2 0.0 collective-permute-done.5.rest_1_
  24.2 1.1 %collective-permute-done.6.rest_2_ = bf16[96,1152]{1,0:T(8,128)(2,1)S(1)} collective-permute-done((bf16[96,1152]{1,0:T(8,128)(2,1)S(1)}, bf16[96,1152]{1,0:T(8,128)(2,1)S(1)}, u32[]{:S(2)}, u32[]{:S(2)}) %collective-permute-start.6) | collective-permute-done | bytes 221216 | tf_op jit(solution)/shard_map/ppermute | solution.py:22
  25.3 1.1 %more.4.dir_ref = f32[2,192,1152]{2,1,0:T(8,128)S(1)} custom-call(f32[8,128]{1,0:T(8,128)S(1)} %get-tuple-element.21.scale_ref, bf16[2,192,1152]{2,1,0:T(8,128)(2,1)S(1)} %get-tuple-element.22.half_ref, f32[2,192,1152]{2,1,0:T(8,128)S(1)} %get-tuple-element.24.dir_ref, ...), custom_call_target="tpu_custom_call", output_to_operand_aliasing={{}: (2, {})} | custom-call | flops 1000 | bytes 1000 | tf_op jit(solution)/shard_map/more/pallas_call | solution.py:282
  26.4 0.0 collective-permute-done.2.raw_ref
  26.4 0.2 unit.1.rest_2_
  26.6 0.0 collective-permute-done.1.rest_1_
  26.6 0.6 %collective-permute-start.7 = (bf16[192,1152]{1,0:T(8,128)(2,1)S(1)}, bf16[192,1152]{1,0:T(8,128)(2,1)S(1)}, u32[]{:S(2)}, u32[]{:S(2)}) collective-permute-start(bf16[192,1152]{1,0:T(8,128)(2,1)S(1)} %collective-permute-done.rest_0_), channel_id=1, source_target_pairs={{0,4},{4,0},{8,12},{12,8},{16,20},{20,16},{24,28},{28,24},{1,5},{5... | collective-permute-start | bytes 1327112 | tf_op jit(solution)/shard_map/ppermute | solution.py:22
  27.3 0.1 collective-permute-start.8
  27.3 1.7 %more.5.dir_ref = f32[2,192,1152]{2,1,0:T(8,128)S(1)} custom-call(f32[8,128]{1,0:T(8,128)S(1)} %get-tuple-element.21.scale_ref, bf16[2,192,1152]{2,1,0:T(8,128)(2,1)S(1)} %get-tuple-element.22.half_ref, f32[2,192,1152]{2,1,0:T(8,128)S(1)} %more.4.dir_ref, bf16[192,1152]{1,0:T(8,128)(2,1)S(1)} %collective-permute-done.rest_0_, ...), custom_call_target="tpu_custom_call", output_to_operand_aliasing={{}: (2, {})} | custom-call | flops 1000 | bytes 1000 | tf_op jit(solution)/shard_map/more/pallas_call | solution.py:282
  29.0 0.0 collective-permute-done.7.rest_0_
  29.0 0.3 collective-permute-done.8.rest_1_
  29.3 2.7 %last.1 = (f32[192,1152]{1,0:T(8,128)}, f32[192,1152]{1,0:T(8,128)}) custom-call(f32[8,128]{1,0:T(8,128)S(1)} %get-tuple-element.21.scale_ref, bf16[2,192,1152]{2,1,0:T(8,128)(2,1)S(1)} %get-tuple-element.22.half_ref, f32[2,192,1152]{2,1,0:T(8,128)S(1)} %more.5.dir_ref, bf16[2,192,1152]{2,1,0:T(8,128)(2,1)S(1)} %get-tuple-element.34.raw_ref, ...), custom_call_target="tpu_custom_call" | custom-call | flops 1000 | bytes 1000 | tf_op jit(solution)/shard_map/last/pallas_call | solution.py:306
  (2 shorter events, 0.0 us)
Async XLA Ops:
  0.6 12.0 %collective-permute-start.3 = (bf16[192,1152]{1,0:T(8,128)(2,1)}, bf16[192,1152]{1,0:T(8,128)(2,1)S(1)}, u32[]{:S(2)}, u32[]{:S(2)}) collective-permute-start(bf16[192,1152]{1,0:T(8,128)(2,1)} %txt_ref.5), channel_id=1, source_target_pairs={{0,8},{4,12},{8,16},{12,20},{16,24},{20,28},{24,0},{28,4},{1,9},{5... | collective-permute-start | bytes 1327112 | tf_op jit(solution)/shard_map/ppermute | solution.py:22
  1.9 13.8 %collective-permute-start.4 = (bf16[192,1152]{1,0:T(8,128)(2,1)}, bf16[192,1152]{1,0:T(8,128)(2,1)S(1)}, u32[]{:S(2)}, u32[]{:S(2)}) collective-permute-start(bf16[192,1152]{1,0:T(8,128)(2,1)} %txt_ref.5), channel_id=1, source_target_pairs={{0,1},{1,2},{2,3},{3,0},{4,5},{5,6},{6,7},{7,4},{8,9},{9,10},{10,1... | collective-permute-start | bytes 1327112 | tf_op jit(solution)/shard_map/ppermute | solution.py:22
  4.3 22.1 %collective-permute-start.2 = (bf16[192,1152]{1,0:T(8,128)(2,1)S(1)}, bf16[192,1152]{1,0:T(8,128)(2,1)S(1)}, u32[]{:S(2)}, u32[]{:S(2)}) collective-permute-start(bf16[192,1152]{1,0:T(8,128)(2,1)S(1)} %pick.1), channel_id=1, source_target_pairs={{0,20},{4,16},{8,28},{12,24},{16,4},{20,0},{24,12},{28,8},{1,21},{... | collective-permute-start | bytes 1327112 | tf_op jit(solution)/shard_map/ppermute | solution.py:22
  7.6 19.0 %collective-permute-start = (bf16[192,1152]{1,0:T(8,128)(2,1)S(1)}, bf16[192,1152]{1,0:T(8,128)(2,1)S(1)}, u32[]{:S(2)}, u32[]{:S(2)}) collective-permute-start(bf16[192,1152]{1,0:T(8,128)(2,1)S(1)} %get-tuple-element.19.img_half), channel_id=1, source_target_pairs={{0,24},{4,28},{8,0},{12,4},{16,8},{20,12},{24,16},{28,20},{1,25},{... | collective-permute-start | bytes 1327112 | tf_op jit(solution)/shard_map/ppermute | solution.py:22
  8.9 17.7 %collective-permute-start.1 = (bf16[192,1152]{1,0:T(8,128)(2,1)S(1)}, bf16[192,1152]{1,0:T(8,128)(2,1)S(1)}, u32[]{:S(2)}, u32[]{:S(2)}) collective-permute-start(bf16[192,1152]{1,0:T(8,128)(2,1)S(1)} %get-tuple-element.19.img_half), channel_id=1, source_target_pairs={{0,3},{1,0},{2,1},{3,2},{4,7},{5,4},{6,5},{7,6},{8,11},{9,8},{10,9... | collective-permute-start | bytes 1327112 | tf_op jit(solution)/shard_map/ppermute | solution.py:22
  13.7 10.5 %collective-permute-start.5 = (bf16[96,1152]{1,0:T(8,128)(2,1)S(1)}, bf16[96,1152]{1,0:T(8,128)(2,1)S(1)}, u32[]{:S(2)}, u32[]{:S(2)}) collective-permute-start(bf16[96,1152]{1,0:T(8,128)(2,1)S(1)} %get-tuple-element.25), channel_id=1, source_target_pairs={{0,4},{4,0},{8,12},{12,8},{16,20},{20,16},{24,28},{28,24},{1,5},{5... | collective-permute-start | bytes 663560 | tf_op jit(solution)/shard_map/ppermute | solution.py:22
  15.7 9.6 %collective-permute-start.6 = (bf16[96,1152]{1,0:T(8,128)(2,1)S(1)}, bf16[96,1152]{1,0:T(8,128)(2,1)S(1)}, u32[]{:S(2)}, u32[]{:S(2)}) collective-permute-start(bf16[96,1152]{1,0:T(8,128)(2,1)S(1)} %get-tuple-element.26), channel_id=1, source_target_pairs={{0,4},{4,0},{8,12},{12,8},{16,20},{20,16},{24,28},{28,24},{1,5},{5... | collective-permute-start | bytes 663560 | tf_op jit(solution)/shard_map/ppermute | solution.py:22
  26.6 2.4 %collective-permute-start.7 = (bf16[192,1152]{1,0:T(8,128)(2,1)S(1)}, bf16[192,1152]{1,0:T(8,128)(2,1)S(1)}, u32[]{:S(2)}, u32[]{:S(2)}) collective-permute-start(bf16[192,1152]{1,0:T(8,128)(2,1)S(1)} %collective-permute-done.rest_0_), channel_id=1, source_target_pairs={{0,4},{4,0},{8,12},{12,8},{16,20},{20,16},{24,28},{28,24},{1,5},{5... | collective-permute-start | bytes 1327112 | tf_op jit(solution)/shard_map/ppermute | solution.py:22
  27.3 2.1 %collective-permute-start.8 = (bf16[192,1152]{1,0:T(8,128)(2,1)S(1)}, bf16[192,1152]{1,0:T(8,128)(2,1)S(1)}, u32[]{:S(2)}, u32[]{:S(2)}) collective-permute-start(bf16[192,1152]{1,0:T(8,128)(2,1)S(1)} %get-tuple-element.35), channel_id=1, source_target_pairs={{0,4},{4,0},{8,12},{12,8},{16,20},{20,16},{24,28},{28,24},{1,5},{5... | collective-permute-start | bytes 1327112 | tf_op jit(solution)/shard_map/ppermute | solution.py:22

commit v2 on v1

--- a/solution.py
+++ b/solution.py
@@ -13,7 +13,7 @@
 HBM = pl.BlockSpec(memory_space=pltpu.HBM)
 LIMIT = 24 * 2**20
 PIECES = 4
-CUTS = 2
+CUTS = 1
 
 
 def along(value, axis, target):
@@ -68,14 +68,14 @@
     ]
 
 
-def call(kernel, out_shape, in_specs, out_specs, **more):
+def call(kernel, out_shape, in_specs, out_specs, work=1000, **more):
     return pl.pallas_call(
         kernel,
         out_shape=out_shape,
         in_specs=in_specs,
         out_specs=out_specs,
         compiler_params=pltpu.CompilerParams(vmem_limit_bytes=LIMIT),
-        cost_estimate=pl.CostEstimate(flops=1000, bytes_accessed=1000, transcendentals=0),
+        cost_estimate=pl.CostEstimate(flops=work, bytes_accessed=work, transcendentals=0),
         **more,
     )
 
@@ -214,27 +214,29 @@
 def visit_all(kinds, blocks, scale_ref, half_ref, dir_ref, acc_ref, others_ref, sides=(0, 1)):
     rows = half_ref.shape[1]
     blocks = parts_of(kinds, blocks, rows)
-    held = [others_ref.at[pl.ds(n * rows, rows)] for n in range(len(kinds))]
-    order = sorted(range(len(kinds)), key=lambda n: kinds[n][0])
-    for place, n in enumerate(order):
-        start = 0
-        for part in blocks[n]:
+    pairs = sum(side == 2 for side, _ in kinds)
+    counts = [sum(kind[0] == side for kind in kinds) + pairs for side in (0, 1)]
+    placed = [0, 0, 0, 0]
+    for (side, raw), block in zip(kinds, blocks):
+        if side < 2:
+            slot = side * counts[0] + placed[side]
+        else:
+            to = odd_row() if side == 2 else 1 - odd_row()
+            ends = [counts[0] - pairs + placed[side], sum(counts) - pairs + placed[side]]
+            slot = ends[0] + to * (ends[1] - ends[0])
+        placed[side] += 1
+        start = slot * rows
+        for part in block:
             size = part.shape[0]
-            block = part[...]
-            held[place][pl.ds(start, size)] = unit_half(block) if kinds[n][1] else block
+            at = start if isinstance(start, int) else pl.multiple_of(start, 16)
+            others_ref[pl.ds(at, size)] = unit_half(part[...]) if raw else part[...]
             start += size
-    first = 0
     for side in sides:
-        count = sum(kind[0] == side for kind in kinds)
-        if count:
-            others = others_ref[pl.ds(first * rows, count * rows)]
+        if counts[side]:
+            others = others_ref[pl.ds(side * counts[0] * rows, counts[side] * rows)]
             acc_ref[side] = dir_ref[side] + visit(half_ref[side], others, scale_ref)
         else:
             acc_ref[side] = dir_ref[side]
-        first += count
-    for place in range(first, len(kinds)):
-        at = odd_row() if kinds[order[place]][0] == 2 else 1 - odd_row()
-        acc_ref[at] += visit(half_ref[at], held[place][...], scale_ref)
 
 
 def more_kernel(kinds, given, scale_ref, half_ref, dir_ref, *rest):
@@ -259,22 +261,19 @@
 
 def last_kernel(kinds, scale_ref, half_ref, dir_ref, raw_ref, *rest):
     blocks, (img_grad, txt_grad, acc_ref, others_ref, held_ref, sems) = rest[:-6], rest[-6:]
-    texts = [n for n, (side, _) in enumerate(kinds) if side == 1]
-    late = [(kinds[n], blocks[n]) for n in texts]
-    early = [(kinds[n], blocks[n]) for n in range(len(kinds)) if n not in texts]
-    copies, source = [], dir_ref
-    for side, entries, grad_ref in ((0, early, img_grad), (1, late, txt_grad)):
-        sides = (0, 1) if side == 0 else (1,)
-        visit_all(*flat(entries), scale_ref, half_ref, source, acc_ref, others_ref, sides)
-        copies += finish(
-            raw_ref.at[side], acc_ref.at[side], grad_ref, held_ref.at[side], sems.at[side]
-        )
-        source = acc_ref
+    texts = any(side == 0 for side, _ in kinds)
+    if texts:
+        visit_all(kinds, blocks, scale_ref, half_ref, dir_ref, acc_ref, others_ref)
+    source = acc_ref if texts else dir_ref
+    copies = finish(raw_ref.at[0], source.at[0], img_grad, held_ref.at[0], sems.at[0])
+    if not texts:
+        visit_all(kinds, blocks, scale_ref, half_ref, dir_ref, acc_ref, others_ref, (1,))
+    copies += finish(raw_ref.at[1], acc_ref.at[1], txt_grad, held_ref.at[1], sems.at[1])
     for copy in copies:
         copy.wait()
 
 
-def more_visits(scale, half, direction, entries, give=False):
+def more_visits(scale, half, direction, entries, give=False, work=1000):
     kinds, blocks = flat(entries)
     rows, width = half.shape[1:]
     one = jax.ShapeDtypeStruct((rows, width), jnp.bfloat16)
@@ -286,6 +285,7 @@
         (VMEM,) * (1 + len(halves)),
         scratch_shapes=[pltpu.VMEM((len(kinds) * rows, width), jnp.bfloat16)],
         input_output_aliases={2: 0},
+        work=work,
         name="more",
     )(scale, half, direction, *blocks)
     return (direction, halves) if give else direction
@@ -359,14 +359,15 @@
         for n in range(len(text_rows)):
             block = halves[n * per : (n + 1) * per]
             swapped.append(((0, False), [along(cut, "row", swap) for cut in block]))
-    if text_cols + swapped:
-        direction = more_visits(scale, half, direction, text_cols + swapped)
+    near, direction = lax.optimization_barrier((near, direction))
+    swapped.append(((3, False), along(near, "row", swap)))
+    if text_cols:
+        direction = more_visits(scale, half, direction, text_cols)
     far, direction = lax.optimization_barrier((far, direction))
     middle = image_rows + image_cols + [((2, False), normalized(far))]
-    middle, near, direction = tied(middle, near, direction)
+    middle, direction = tied(middle, direction)
     last = [(kind, along(block, "row", swap)) for kind, block in middle[: len(image_rows)]]
-    last.append(((3, False), along(near, "row", swap)))
-    direction = more_visits(scale, half, direction, middle)
+    direction = more_visits(scale, half, direction, middle + swapped, work=4000000)
     return last_visits(scale, half, direction, raw, last)
 
 

time: 32.2 us -> 31.8 us (0.988)
  waiting for transfers between devices: 1.41 us -> 0.99 us
    pallas_call x1, Pallas kernels: 2.66 us -> 2.15 us  [last_visits(): call(functools.partial(last_kernel, kinds), (grad, grad), [VMEM] * (4 + l...]
    ppermute x9 -> x8, waiting for transfers between devices: 1.41 us -> 0.99 us  [along(): return lax.ppermute(value, axis, pairs)]
    ppermute x9 -> x8, starting transfers between devices: 16.7 us -> 16.9 us  [along(): return lax.ppermute(value, axis, pairs)]
  transfers between devices with their start and end apart: 9 -> 8, of which waited for: 2 -> 1; matrix products, arithmetic and copies ran while one was open for 0% -> 0% of each run, Pallas kernels for 29% -> 30%
where the time goes in v2:
time: 31.8 us; the launch traced here: 31.5 us
  starting transfers between devices  16.9 us (53%)
  Pallas kernels  11.6 us (36%)
  between operations  2.01 us (6%)
  waiting for transfers between devices  0.99 us (3%)
    ppermute x8, starting transfers between devices, along(): return lax.ppermute(value, axis, pairs)  16.9 us
    pallas_call x3, Pallas kernels, more_visits(): call(functools.partial(more_kernel, kinds, len(halves)), (jax.ShapeDtypeS...  4.06 us
    pallas_call x1, Pallas kernels, own_visit(): call(own_kernel, (jax.ShapeDtypeStruct((8, 128), jnp.float32), both, both...  2.27 us
    pallas_call x1, Pallas kernels, last_visits(): call(functools.partial(last_kernel, kinds), (grad, grad), [VMEM] * (4 + l...  2.15 us
    pallas_call x1, Pallas kernels, norm(): call(norm_kernel, (one, one), [HBM, HBM], (VMEM, VMEM), scratch_shapes=[p...  1.87 us
    pallas_call x1, Pallas kernels, pick(): call(pick_kernel, jax.ShapeDtypeStruct(img.shape, img.dtype), [HBM, HBM],...  1.09 us
    ppermute x8, waiting for transfers between devices, along(): return lax.ppermute(value, axis, pairs)  0.99 us
  transfers between devices with their start and end apart: 8, of which 1 were waited for; matrix products, arithmetic and copies ran while one was open for 0% of the time, Pallas kernels for 30%

profile of v2, /device:TPU:19, one launch (start us, length us, event | category | flops | bytes accessed | tf_op | source)
XLA Modules:
  0.0 31.5 jit_solution(1408060879576353545)
XLA Ops:
  0.6 1.3 %collective-permute-start.3 = (bf16[192,1152]{1,0:T(8,128)(2,1)}, bf16[192,1152]{1,0:T(8,128)(2,1)S(1)}, u32[]{:S(2)}, u32[]{:S(2)}) collective-permute-start(bf16[192,1152]{1,0:T(8,128)(2,1)} %txt_ref.5), channel_id=1, source_target_pairs={{0,8},{4,12},{8,16},{12,20},{16,24},{20,28},{24,0},{28,4},{1,9},{5... | collective-permute-start | bytes 1327112 | tf_op jit(solution)/shard_map/ppermute | solution.py:22
  1.9 1.3 %collective-permute-start.4 = (bf16[192,1152]{1,0:T(8,128)(2,1)}, bf16[192,1152]{1,0:T(8,128)(2,1)S(1)}, u32[]{:S(2)}, u32[]{:S(2)}) collective-permute-start(bf16[192,1152]{1,0:T(8,128)(2,1)} %txt_ref.5), channel_id=1, source_target_pairs={{0,1},{1,2},{2,3},{3,0},{4,5},{5,6},{6,7},{7,4},{8,9},{9,10},{10,1... | collective-permute-start | bytes 1327112 | tf_op jit(solution)/shard_map/ppermute | solution.py:22
  3.2 1.1 %pick.1 = bf16[192,1152]{1,0:T(8,128)(2,1)S(1)} custom-call(bf16[192,1152]{1,0:T(8,128)(2,1)} %img_ref.5, bf16[192,1152]{1,0:T(8,128)(2,1)} %txt_ref.5), custom_call_target="tpu_custom_call" | custom-call | flops 1000 | bytes 1000 | tf_op jit(solution)/shard_map/pick/pallas_call | solution.py:107
  4.3 1.4 %collective-permute-start.2 = (bf16[192,1152]{1,0:T(8,128)(2,1)S(1)}, bf16[192,1152]{1,0:T(8,128)(2,1)S(1)}, u32[]{:S(2)}, u32[]{:S(2)}) collective-permute-start(bf16[192,1152]{1,0:T(8,128)(2,1)S(1)} %pick.1), channel_id=1, source_target_pairs={{0,20},{4,16},{8,28},{12,24},{16,4},{20,0},{24,12},{28,8},{1,21},{... | collective-permute-start | bytes 1327112 | tf_op jit(solution)/shard_map/ppermute | solution.py:22
  5.7 1.9 %norm.1 = (bf16[192,1152]{1,0:T(8,128)(2,1)S(1)}, bf16[192,1152]{1,0:T(8,128)(2,1)S(1)}) custom-call(bf16[192,1152]{1,0:T(8,128)(2,1)} %img_ref.5, bf16[192,1152]{1,0:T(8,128)(2,1)} %txt_ref.5), custom_call_target="tpu_custom_call" | custom-call | flops 1000 | bytes 1000 | tf_op jit(solution)/shard_map/norm/pallas_call | solution.py:142
  7.6 1.3 %collective-permute-start = (bf16[192,1152]{1,0:T(8,128)(2,1)S(1)}, bf16[192,1152]{1,0:T(8,128)(2,1)S(1)}, u32[]{:S(2)}, u32[]{:S(2)}) collective-permute-start(bf16[192,1152]{1,0:T(8,128)(2,1)S(1)} %get-tuple-element.19.img_half), channel_id=1, source_target_pairs={{0,24},{4,28},{8,0},{12,4},{16,8},{20,12},{24,16},{28,20},{1,25},{... | collective-permute-start | bytes 1327112 | tf_op jit(solution)/shard_map/ppermute | solution.py:22
  8.9 0.2 collective-permute-start.1
  10.4 2.3 %own.1 = (f32[8,128]{1,0:T(8,128)S(1)}, bf16[2,192,1152]{2,1,0:T(8,128)(2,1)S(1)}, bf16[2,192,1152]{2,1,0:T(8,128)(2,1)S(1)}, bf16[192,1152]{1,0:T(8,128)(2,1)S(1)}, f32[2,192,1152]{2,1,0:T(8,128)S(1)}) custom-call(f32[1,1]{1,0:T(1,128)} %bitcast.2.exponent_ref, f32[1,1]{1,0:T(1,128)} %bitcast.3.offset_ref, bf16[192,1152]{1,0:T(8,128)(2,1)} %img_ref.5, ...), custom_call_target="tpu_custom_call" | custom-call | flops 1000 | bytes 1000 | tf_op jit(solution)/shard_map/own/pallas_call | solution.py:183
  12.7 0.0 collective-permute-done.3.rest_0_
  12.7 1.0 %more.3 = (f32[2,192,1152]{2,1,0:T(8,128)S(1)}, bf16[192,1152]{1,0:T(8,128)(2,1)S(1)}) custom-call(f32[8,128]{1,0:T(8,128)S(1)} %get-tuple-element.21.scale_ref, bf16[2,192,1152]{2,1,0:T(8,128)(2,1)S(1)} %get-tuple-element.22.half_ref, f32[2,192,1152]{2,1,0:T(8,128)S(1)} %get-tuple-element.24.dir_ref, ...), custom_call_target="tpu_custom_call", output_to_operand_aliasing={{0}: (2, {})} | custom-call | flops 1000 | bytes 1000 | tf_op jit(solution)/shard_map/more/pallas_call | solution.py:281
  13.7 2.0 %collective-permute-start.6 = (bf16[192,1152]{1,0:T(8,128)(2,1)S(1)}, bf16[192,1152]{1,0:T(8,128)(2,1)S(1)}, u32[]{:S(2)}, u32[]{:S(2)}) collective-permute-start(bf16[192,1152]{1,0:T(8,128)(2,1)S(1)} %get-tuple-element.34), channel_id=1, source_target_pairs={{0,4},{4,0},{8,12},{12,8},{16,20},{20,16},{24,28},{28,24},{1,5},{5... | collective-permute-start | bytes 1327112 | tf_op jit(solution)/shard_map/ppermute | solution.py:22
  15.7 0.0 collective-permute-done.4.rest_0_
  15.7 8.5 %collective-permute-start.5 = (bf16[192,1152]{1,0:T(8,128)(2,1)S(1)}, bf16[192,1152]{1,0:T(8,128)(2,1)S(1)}, u32[]{:S(2)}, u32[]{:S(2)}) collective-permute-start(bf16[192,1152]{1,0:T(8,128)(2,1)S(1)} %get-tuple-element.33), channel_id=1, source_target_pairs={{0,4},{4,0},{8,12},{12,8},{16,20},{20,16},{24,28},{28,24},{1,5},{5... | collective-permute-start | bytes 1327112 | tf_op jit(solution)/shard_map/ppermute | solution.py:22
  24.2 1.0 %more.4.dir_ref = f32[2,192,1152]{2,1,0:T(8,128)S(1)} custom-call(f32[8,128]{1,0:T(8,128)S(1)} %get-tuple-element.21.scale_ref, bf16[2,192,1152]{2,1,0:T(8,128)(2,1)S(1)} %get-tuple-element.22.half_ref, f32[2,192,1152]{2,1,0:T(8,128)S(1)} %get-tuple-element.26.dir_ref, ...), custom_call_target="tpu_custom_call", output_to_operand_aliasing={{}: (2, {})} | custom-call | flops 1000 | bytes 1000 | tf_op jit(solution)/shard_map/more/pallas_call | solution.py:281
  25.1 1.0 %collective-permute-done.2.raw_ref = bf16[192,1152]{1,0:T(8,128)(2,1)S(1)} collective-permute-done((bf16[192,1152]{1,0:T(8,128)(2,1)S(1)}, bf16[192,1152]{1,0:T(8,128)(2,1)S(1)}, u32[]{:S(2)}, u32[]{:S(2)}) %collective-permute-start.2) | collective-permute-done | bytes 442400 | tf_op jit(solution)/shard_map/ppermute | solution.py:22
  26.1 0.2 unit.1.rest_2_
  26.3 0.0 collective-permute-done.rest_0_
  26.3 0.0 collective-permute-done.1.rest_1_
  26.3 0.9 %collective-permute-start.7 = (bf16[192,1152]{1,0:T(8,128)(2,1)S(1)}, bf16[192,1152]{1,0:T(8,128)(2,1)S(1)}, u32[]{:S(2)}, u32[]{:S(2)}) collective-permute-start(bf16[192,1152]{1,0:T(8,128)(2,1)S(1)} %collective-permute-done.rest_0_), channel_id=1, source_target_pairs={{0,4},{4,0},{8,12},{12,8},{16,20},{20,16},{24,28},{28,24},{1,5},{5... | collective-permute-start | bytes 1327112 | tf_op jit(solution)/shard_map/ppermute | solution.py:22
  27.3 0.0 collective-permute-done.6.rest_4_
  27.3 0.0 collective-permute-done.5.rest_3_
  27.3 2.1 %more.5.dir_ref = f32[2,192,1152]{2,1,0:T(8,128)S(1)} custom-call(f32[8,128]{1,0:T(8,128)S(1)} %get-tuple-element.21.scale_ref, bf16[2,192,1152]{2,1,0:T(8,128)(2,1)S(1)} %get-tuple-element.22.half_ref, f32[2,192,1152]{2,1,0:T(8,128)S(1)} %more.4.dir_ref, bf16[192,1152]{1,0:T(8,128)(2,1)S(1)} %collective-permute-done.rest_0_, ...), custom_call_target="tpu_custom_call", output_to_operand_aliasing={{}: (2, {})} | custom-call | flops 4000000 | bytes 4000000 | tf_op jit(solution)/shard_map/more/pallas_call | solution.py:281
  29.4 0.0 collective-permute-done.7.rest_0_
  29.4 2.2 %last.1 = (f32[192,1152]{1,0:T(8,128)}, f32[192,1152]{1,0:T(8,128)}) custom-call(f32[8,128]{1,0:T(8,128)S(1)} %get-tuple-element.21.scale_ref, bf16[2,192,1152]{2,1,0:T(8,128)(2,1)S(1)} %get-tuple-element.22.half_ref, f32[2,192,1152]{2,1,0:T(8,128)S(1)} %more.5.dir_ref, bf16[2,192,1152]{2,1,0:T(8,128)(2,1)S(1)} %get-tuple-element.35.raw_ref, ...), custom_call_target="tpu_custom_call" | custom-call | flops 1000 | bytes 1000 | tf_op jit(solution)/shard_map/last/pallas_call | solution.py:306
Async XLA Ops:
  0.6 12.0 %collective-permute-start.3 = (bf16[192,1152]{1,0:T(8,128)(2,1)}, bf16[192,1152]{1,0:T(8,128)(2,1)S(1)}, u32[]{:S(2)}, u32[]{:S(2)}) collective-permute-start(bf16[192,1152]{1,0:T(8,128)(2,1)} %txt_ref.5), channel_id=1, source_target_pairs={{0,8},{4,12},{8,16},{12,20},{16,24},{20,28},{24,0},{28,4},{1,9},{5... | collective-permute-start | bytes 1327112 | tf_op jit(solution)/shard_map/ppermute | solution.py:22
  1.9 13.8 %collective-permute-start.4 = (bf16[192,1152]{1,0:T(8,128)(2,1)}, bf16[192,1152]{1,0:T(8,128)(2,1)S(1)}, u32[]{:S(2)}, u32[]{:S(2)}) collective-permute-start(bf16[192,1152]{1,0:T(8,128)(2,1)} %txt_ref.5), channel_id=1, source_target_pairs={{0,1},{1,2},{2,3},{3,0},{4,5},{5,6},{6,7},{7,4},{8,9},{9,10},{10,1... | collective-permute-start | bytes 1327112 | tf_op jit(solution)/shard_map/ppermute | solution.py:22
  4.3 21.8 %collective-permute-start.2 = (bf16[192,1152]{1,0:T(8,128)(2,1)S(1)}, bf16[192,1152]{1,0:T(8,128)(2,1)S(1)}, u32[]{:S(2)}, u32[]{:S(2)}) collective-permute-start(bf16[192,1152]{1,0:T(8,128)(2,1)S(1)} %pick.1), channel_id=1, source_target_pairs={{0,20},{4,16},{8,28},{12,24},{16,4},{20,0},{24,12},{28,8},{1,21},{... | collective-permute-start | bytes 1327112 | tf_op jit(solution)/shard_map/ppermute | solution.py:22
  7.6 18.7 %collective-permute-start = (bf16[192,1152]{1,0:T(8,128)(2,1)S(1)}, bf16[192,1152]{1,0:T(8,128)(2,1)S(1)}, u32[]{:S(2)}, u32[]{:S(2)}) collective-permute-start(bf16[192,1152]{1,0:T(8,128)(2,1)S(1)} %get-tuple-element.19.img_half), channel_id=1, source_target_pairs={{0,24},{4,28},{8,0},{12,4},{16,8},{20,12},{24,16},{28,20},{1,25},{... | collective-permute-start | bytes 1327112 | tf_op jit(solution)/shard_map/ppermute | solution.py:22
  8.9 17.4 %collective-permute-start.1 = (bf16[192,1152]{1,0:T(8,128)(2,1)S(1)}, bf16[192,1152]{1,0:T(8,128)(2,1)S(1)}, u32[]{:S(2)}, u32[]{:S(2)}) collective-permute-start(bf16[192,1152]{1,0:T(8,128)(2,1)S(1)} %get-tuple-element.19.img_half), channel_id=1, source_target_pairs={{0,3},{1,0},{2,1},{3,2},{4,7},{5,4},{6,5},{7,6},{8,11},{9,8},{10,9... | collective-permute-start | bytes 1327112 | tf_op jit(solution)/shard_map/ppermute | solution.py:22
  13.7 13.6 %collective-permute-start.6 = (bf16[192,1152]{1,0:T(8,128)(2,1)S(1)}, bf16[192,1152]{1,0:T(8,128)(2,1)S(1)}, u32[]{:S(2)}, u32[]{:S(2)}) collective-permute-start(bf16[192,1152]{1,0:T(8,128)(2,1)S(1)} %get-tuple-element.34), channel_id=1, source_target_pairs={{0,4},{4,0},{8,12},{12,8},{16,20},{20,16},{24,28},{28,24},{1,5},{5... | collective-permute-start | bytes 1327112 | tf_op jit(solution)/shard_map/ppermute | solution.py:22
  15.7 11.6 %collective-permute-start.5 = (bf16[192,1152]{1,0:T(8,128)(2,1)S(1)}, bf16[192,1152]{1,0:T(8,128)(2,1)S(1)}, u32[]{:S(2)}, u32[]{:S(2)}) collective-permute-start(bf16[192,1152]{1,0:T(8,128)(2,1)S(1)} %get-tuple-element.33), channel_id=1, source_target_pairs={{0,4},{4,0},{8,12},{12,8},{16,20},{20,16},{24,28},{28,24},{1,5},{5... | collective-permute-start | bytes 1327112 | tf_op jit(solution)/shard_map/ppermute | solution.py:22
  26.3 3.1 %collective-permute-start.7 = (bf16[192,1152]{1,0:T(8,128)(2,1)S(1)}, bf16[192,1152]{1,0:T(8,128)(2,1)S(1)}, u32[]{:S(2)}, u32[]{:S(2)}) collective-permute-start(bf16[192,1152]{1,0:T(8,128)(2,1)S(1)} %collective-permute-done.rest_0_), channel_id=1, source_target_pairs={{0,4},{4,0},{8,12},{12,8},{16,20},{20,16},{24,28},{28,24},{1,5},{5... | collective-permute-start | bytes 1327112 | tf_op jit(solution)/shard_map/ppermute | solution.py:22

commit v3 on v2

--- a/solution.py
+++ b/solution.py
@@ -13,6 +13,7 @@
 HBM = pl.BlockSpec(memory_space=pltpu.HBM)
 LIMIT = 24 * 2**20
 PIECES = 4
+LOG2_E = 1.4426950408889634
 CUTS = 1
 
 
@@ -39,7 +40,11 @@
 
 
 def visit(own, other, scale_ref):
-    weights = scale_ref[0:1, 0:1] * weigh(own, other, scale_ref)
+    scores = lax.dot_general(
+        own, other, (((1,), (1,)), ((), ())), preferred_element_type=jnp.float32
+    )
+    power = jnp.exp2(scale_ref[2:3, 0:1] * scores + scale_ref[3:4, 0:1])
+    weights = scale_ref[0:1, 0:1] * pl.reciprocal(1.0 + power, approx=False)
     return jnp.dot(weights.astype(jnp.bfloat16), other, preferred_element_type=jnp.float32)
 
 
@@ -47,12 +52,10 @@
     return lax.axis_index("row") & 1
 
 
-def unit_back(raw, direction):
+def unit_back(raw, inverse, direction):
     values = raw.astype(jnp.float32)
-    inverse = inverse_norm(values)
-    unit = values * inverse
-    share = jnp.sum(unit * direction, axis=-1, keepdims=True)
-    return inverse * (direction - unit * share)
+    share = inverse * jnp.sum(values * direction, axis=-1, keepdims=True)
+    return inverse * direction - values * (inverse * inverse * share)
 
 
 def pieces(rows, count=PIECES):
@@ -127,40 +130,44 @@
     return started
 
 
-def norm_kernel(img_ref, txt_ref, img_half, txt_half, raw_ref, sems):
-    halves = (img_half, txt_half)
-    started = load((img_ref, txt_ref), (raw_ref.at[0], raw_ref.at[1]), sems)
-    for side, copies in enumerate(started):
-        for at, copy in copies:
-            copy.wait()
-            halves[side][at] = unit_half(raw_ref[side, at])
-
-
-def norm(img, txt):
-    rows, width = img.shape
-    one = jax.ShapeDtypeStruct((rows, width), jnp.bfloat16)
+def norm_kernel(img_ref, img_half, raw_ref, sems):
+    for at, copy in load((img_ref,), (raw_ref,), sems)[0]:
+        copy.wait()
+        img_half[at] = unit_half(raw_ref[at])
+
+
+def norm(img):
+    one = jax.ShapeDtypeStruct(img.shape, jnp.bfloat16)
     return call(
         norm_kernel,
-        (one, one),
-        [HBM, HBM],
-        (VMEM, VMEM),
+        one,
+        [HBM],
+        VMEM,
         scratch_shapes=[
-            pltpu.VMEM((2, rows, width), jnp.bfloat16),
-            pltpu.SemaphoreType.DMA((2, len(pieces(rows)))),
+            pltpu.VMEM(img.shape, jnp.bfloat16),
+            pltpu.SemaphoreType.DMA((1, len(pieces(img.shape[0])))),
         ],
         name="norm",
-    )(img, txt)
+    )(img)
 
 
 def own_kernel(
-    exponent_ref, offset_ref, img_ref, txt_ref, img_half, txt_half,
-    scale_ref, raw_ref, half_ref, near_ref, dir_ref, sems,
+    exponent_ref, offset_ref, img_ref, txt_ref, img_half,
+    scale_ref, raw_ref, half_ref, inverse_ref, near_ref, dir_ref, sems,
 ):
     started = load((img_ref, txt_ref), (raw_ref.at[0], raw_ref.at[1]), sems)
     scale_ref[0:1] = jnp.exp(jnp.broadcast_to(exponent_ref[...], (1, 128)))
     scale_ref[1:2] = jnp.broadcast_to(offset_ref[...], (1, 128))
+    scale_ref[2:4] = -LOG2_E * scale_ref[0:2]
     half_ref[0] = img_half[...]
-    half_ref[1] = txt_half[...]
+    for side in (1, 0):
+        for at, copy in started[side]:
+            copy.wait()
+            values = raw_ref[side, at].astype(jnp.float32)
+            inverse = inverse_norm(values)
+            inverse_ref[side, at] = jnp.broadcast_to(inverse, (values.shape[0], 128))
+            if side == 1:
+                half_ref[1, at] = (values * inverse).astype(jnp.bfloat16)
     near_ref[...] = half_ref[1 - odd_row()]
     img, txt = half_ref[0], half_ref[1]
     rows = img.shape[0]
@@ -172,12 +179,9 @@
         dir_ref[side] = jnp.dot(
             weights.astype(jnp.bfloat16), other, preferred_element_type=jnp.float32
         )
-    for copies in started:
-        for _, copy in copies:
-            copy.wait()
-
-
-def own_visit(exponent, offset, img, txt, img_half, txt_half):
+
+
+def own_visit(exponent, offset, img, txt, img_half):
     rows, width = img.shape
     both = jax.ShapeDtypeStruct((2, rows, width), jnp.bfloat16)
     return call(
@@ -186,14 +190,15 @@
             jax.ShapeDtypeStruct((8, 128), jnp.float32),
             both,
             both,
+            jax.ShapeDtypeStruct((2, rows, 128), jnp.float32),
             jax.ShapeDtypeStruct((rows, width), jnp.bfloat16),
             jax.ShapeDtypeStruct((2, rows, width), jnp.float32),
         ),
-        [VMEM, VMEM, HBM, HBM, VMEM, VMEM],
-        (VMEM,) * 5,
+        [VMEM, VMEM, HBM, HBM, VMEM],
+        (VMEM,) * 6,
         scratch_shapes=[pltpu.SemaphoreType.DMA((2, len(pieces(rows))))],
         name="own",
-    )(exponent.reshape(1, 1), offset.reshape(1, 1), img, txt, img_half, txt_half)
+    )(exponent.reshape(1, 1), offset.reshape(1, 1), img, txt, img_half)
 
 
 def parts_of(kinds, refs, rows):
@@ -249,26 +254,30 @@
         start += cut.shape[0]
 
 
-def finish(raw_ref, acc_ref, grad_ref, held_ref, sems):
+def finish(raw_ref, inverse_ref, acc_ref, grad_ref, held_ref, sems):
     copies = []
     for n, (start, size) in enumerate(pieces(held_ref.shape[0])):
         at = pl.ds(start, size)
-        held_ref[at] = unit_back(raw_ref[at], acc_ref[at])
+        held_ref[at] = unit_back(raw_ref[at], inverse_ref[at][:, 0:1], acc_ref[at])
         copies.append(pltpu.make_async_copy(held_ref.at[at], grad_ref.at[at], sems.at[n]))
         copies[-1].start()
     return copies
 
 
-def last_kernel(kinds, scale_ref, half_ref, dir_ref, raw_ref, *rest):
+def last_kernel(kinds, scale_ref, half_ref, dir_ref, raw_ref, inverse_ref, *rest):
     blocks, (img_grad, txt_grad, acc_ref, others_ref, held_ref, sems) = rest[:-6], rest[-6:]
     texts = any(side == 0 for side, _ in kinds)
     if texts:
         visit_all(kinds, blocks, scale_ref, half_ref, dir_ref, acc_ref, others_ref)
     source = acc_ref if texts else dir_ref
-    copies = finish(raw_ref.at[0], source.at[0], img_grad, held_ref.at[0], sems.at[0])
+    copies = finish(
+        raw_ref.at[0], inverse_ref.at[0], source.at[0], img_grad, held_ref.at[0], sems.at[0]
+    )
     if not texts:
         visit_all(kinds, blocks, scale_ref, half_ref, dir_ref, acc_ref, others_ref, (1,))
-    copies += finish(raw_ref.at[1], acc_ref.at[1], txt_grad, held_ref.at[1], sems.at[1])
+    copies += finish(
+        raw_ref.at[1], inverse_ref.at[1], acc_ref.at[1], txt_grad, held_ref.at[1], sems.at[1]
+    )
     for copy in copies:
         copy.wait()
 
@@ -299,14 +308,14 @@
     return call(unit_kernel, jax.ShapeDtypeStruct(raw.shape, raw.dtype), [VMEM], VMEM, name="unit")(raw)
 
 
-def last_visits(scale, half, direction, raw, entries):
+def last_visits(scale, half, direction, raw, inverse, entries):
     kinds, blocks = flat(entries)
     rows, width = half.shape[1:]
     grad = jax.ShapeDtypeStruct((rows, width), jnp.float32)
     return call(
         functools.partial(last_kernel, kinds),
         (grad, grad),
-        [VMEM] * (4 + len(blocks)),
+        [VMEM] * (5 + len(blocks)),
         (HBM, HBM),
         scratch_shapes=[
             pltpu.VMEM(direction.shape, direction.dtype),
@@ -315,7 +324,7 @@
             pltpu.SemaphoreType.DMA((2, len(pieces(rows)))),
         ],
         name="last",
-    )(scale, half, direction, raw, *blocks)
+    )(scale, half, direction, raw, inverse, *blocks)
 
 
 def tied(entries, *others):
@@ -335,18 +344,18 @@
     text_cols, image_cols, text_rows, image_rows, swapped, last = [], [], [], [], [], []
     for k in range(1, column_extent):
         text_cols.append(((0, True), along(txt, "col", lambda s: s + k)))
-    img_half, txt_half = norm(*held)
+    img_half = norm(held[0])
     for k in range(1, column_extent):
         image_cols.append(((1, False), along(img_half, "col", lambda s: s - k)))
-    scale, raw, half, near, direction = own_visit(
-        softness_factor_exponent, logit_offset_term, *held, img_half, txt_half
+    scale, raw, half, inverse, near, direction = own_visit(
+        softness_factor_exponent, logit_offset_term, *held, img_half
     )
     if not paired:
         for k in range(1, row_extent):
             text_rows.append(((0, True), along(txt, "row", lambda s: s + k)))
             image_rows.append(((1, False), along(img_half, "row", lambda s: s - k)))
         last = text_cols + image_cols + text_rows + image_rows
-        return last_visits(scale, half, direction, raw, last)
+        return last_visits(scale, half, direction, raw, inverse, last)
 
     reach = row_extent - 1
     far = along(pick(*held), "row", lambda s: s + reach if s % 2 else s - reach)
@@ -368,7 +377,7 @@
     middle, direction = tied(middle, direction)
     last = [(kind, along(block, "row", swap)) for kind, block in middle[: len(image_rows)]]
     direction = more_visits(scale, half, direction, middle + swapped, work=4000000)
-    return last_visits(scale, half, direction, raw, last)
+    return last_visits(scale, half, direction, raw, inverse, last)
 
 
 def solution(mesh):

time: 31.8 us -> 31.5 us (level)
  starting transfers between devices: 16.9 us -> 16.4 us
    pallas_call x1, Pallas kernels: 2.27 us -> 3.31 us  [own_visit(): call(own_kernel, (jax.ShapeDtypeStruct((8, 128), jnp.float32), both, both...]
    pallas_call x2, Pallas kernels: 4.03 us -> 3.39 us  [the longest x1 2.01 us: last_visits(): call(functools.partial(last_kernel, kinds), (grad, grad), [VMEM] * (5 + l...]
    ppermute x8, starting transfers between devices: 16.9 us -> 16.4 us  [along(): return lax.ppermute(value, axis, pairs)]
  transfers between devices with their start and end apart: 8 -> 8, of which waited for: 1 -> 1; matrix products, arithmetic and copies ran while one was open for 0% -> 0% of each run, Pallas kernels for 30% -> 32%
where the time goes in v3:
time: 31.5 us; the launch traced here: 31.3 us
  starting transfers between devices  16.4 us (52%)
  Pallas kernels  11.9 us (38%)
  between operations  2.01 us (6%)
  waiting for transfers between devices  0.98 us (3%)
    ppermute x8, starting transfers between devices, along(): return lax.ppermute(value, axis, pairs)  16.4 us
    pallas_call x3, Pallas kernels, more_visits(): call(functools.partial(more_kernel, kinds, len(halves)), (jax.ShapeDtypeS...  3.98 us
    pallas_call x1, Pallas kernels, own_visit(): call(own_kernel, (jax.ShapeDtypeStruct((8, 128), jnp.float32), both, both...  3.31 us
    pallas_call x1, Pallas kernels, last_visits(): call(functools.partial(last_kernel, kinds), (grad, grad), [VMEM] * (5 + l...  2.01 us
    pallas_call x1, Pallas kernels, norm(): call(norm_kernel, one, [HBM], VMEM, scratch_shapes=[pltpu.VMEM(img.shape,...  1.38 us
    pallas_call x1, Pallas kernels, pick(): call(pick_kernel, jax.ShapeDtypeStruct(img.shape, img.dtype), [HBM, HBM],...  1.09 us
    ppermute x8, waiting for transfers between devices, along(): return lax.ppermute(value, axis, pairs)  0.98 us
  transfers between devices with their start and end apart: 8, of which 1 were waited for; matrix products, arithmetic and copies ran while one was open for 0% of the time, Pallas kernels for 32%

profile of v3, /device:TPU:19, one launch (start us, length us, event | category | flops | bytes accessed | tf_op | source)
XLA Modules:
  0.0 31.3 jit_solution(11892037843577172296)
XLA Ops:
  0.6 1.3 %collective-permute-start.3 = (bf16[192,1152]{1,0:T(8,128)(2,1)}, bf16[192,1152]{1,0:T(8,128)(2,1)S(1)}, u32[]{:S(2)}, u32[]{:S(2)}) collective-permute-start(bf16[192,1152]{1,0:T(8,128)(2,1)} %txt_ref.3), channel_id=1, source_target_pairs={{0,8},{4,12},{8,16},{12,20},{16,24},{20,28},{24,0},{28,4},{1,9},{5... | collective-permute-start | bytes 1327112 | tf_op jit(solution)/shard_map/ppermute | solution.py:23
  1.9 1.3 %collective-permute-start.4 = (bf16[192,1152]{1,0:T(8,128)(2,1)}, bf16[192,1152]{1,0:T(8,128)(2,1)S(1)}, u32[]{:S(2)}, u32[]{:S(2)}) collective-permute-start(bf16[192,1152]{1,0:T(8,128)(2,1)} %txt_ref.3), channel_id=1, source_target_pairs={{0,1},{1,2},{2,3},{3,0},{4,5},{5,6},{6,7},{7,4},{8,9},{9,10},{10,1... | collective-permute-start | bytes 1327112 | tf_op jit(solution)/shard_map/ppermute | solution.py:23
  3.2 1.1 %pick.1 = bf16[192,1152]{1,0:T(8,128)(2,1)S(1)} custom-call(bf16[192,1152]{1,0:T(8,128)(2,1)} %img_ref.5, bf16[192,1152]{1,0:T(8,128)(2,1)} %txt_ref.3), custom_call_target="tpu_custom_call" | custom-call | flops 1000 | bytes 1000 | tf_op jit(solution)/shard_map/pick/pallas_call | solution.py:110
  4.3 1.4 %collective-permute-start.2 = (bf16[192,1152]{1,0:T(8,128)(2,1)S(1)}, bf16[192,1152]{1,0:T(8,128)(2,1)S(1)}, u32[]{:S(2)}, u32[]{:S(2)}) collective-permute-start(bf16[192,1152]{1,0:T(8,128)(2,1)S(1)} %pick.1), channel_id=1, source_target_pairs={{0,20},{4,16},{8,28},{12,24},{16,4},{20,0},{24,12},{28,8},{1,21},{... | collective-permute-start | bytes 1327112 | tf_op jit(solution)/shard_map/ppermute | solution.py:23
  5.7 1.4 %norm.1.img_half = bf16[192,1152]{1,0:T(8,128)(2,1)S(1)} custom-call(bf16[192,1152]{1,0:T(8,128)(2,1)} %img_ref.5), custom_call_target="tpu_custom_call" | custom-call | flops 1000 | bytes 1000 | tf_op jit(solution)/shard_map/norm/pallas_call | solution.py:141
  7.1 1.3 %collective-permute-start = (bf16[192,1152]{1,0:T(8,128)(2,1)S(1)}, bf16[192,1152]{1,0:T(8,128)(2,1)S(1)}, u32[]{:S(2)}, u32[]{:S(2)}) collective-permute-start(bf16[192,1152]{1,0:T(8,128)(2,1)S(1)} %norm.1.img_half), channel_id=1, source_target_pairs={{0,24},{4,28},{8,0},{12,4},{16,8},{20,12},{24,16},{28,20},{1,25},{... | collective-permute-start | bytes 1327112 | tf_op jit(solution)/shard_map/ppermute | solution.py:23
  8.4 0.2 collective-permute-start.1
  9.9 3.3 %own.1 = (f32[8,128]{1,0:T(8,128)S(1)}, bf16[2,192,1152]{2,1,0:T(8,128)(2,1)S(1)}, bf16[2,192,1152]{2,1,0:T(8,128)(2,1)S(1)}, f32[2,192,128]{2,1,0:T(8,128)S(1)}...) custom-call(f32[1,1]{1,0:T(1,128)} %bitcast.2.exponent_ref, f32[1,1]{1,0:T(1,128)} %bitcast.3.offset_ref, ...), custom_call_target="tpu_custom_call" | custom-call | flops 1000 | bytes 1000 | tf_op jit(solution)/shard_map/own/pallas_call | solution.py:187
  13.2 0.0 collective-permute-done.3.rest_0_
  13.2 1.0 %more.3 = (f32[2,192,1152]{2,1,0:T(8,128)S(1)}, bf16[192,1152]{1,0:T(8,128)(2,1)S(1)}) custom-call(f32[8,128]{1,0:T(8,128)S(1)} %get-tuple-element.18.scale_ref, bf16[2,192,1152]{2,1,0:T(8,128)(2,1)S(1)} %get-tuple-element.19.half_ref, f32[2,192,1152]{2,1,0:T(8,128)S(1)} %get-tuple-element.21.dir_ref, ...), custom_call_target="tpu_custom_call", output_to_operand_aliasing={{0}: (2, {})} | custom-call | flops 1000 | bytes 1000 | tf_op jit(solution)/shard_map/more/pallas_call | solution.py:290
  14.2 1.5 %collective-permute-start.6 = (bf16[192,1152]{1,0:T(8,128)(2,1)S(1)}, bf16[192,1152]{1,0:T(8,128)(2,1)S(1)}, u32[]{:S(2)}, u32[]{:S(2)}) collective-permute-start(bf16[192,1152]{1,0:T(8,128)(2,1)S(1)} %get-tuple-element.31), channel_id=1, source_target_pairs={{0,4},{4,0},{8,12},{12,8},{16,20},{20,16},{24,28},{28,24},{1,5},{5... | collective-permute-start | bytes 1327112 | tf_op jit(solution)/shard_map/ppermute | solution.py:23
  15.7 0.0 collective-permute-done.4.rest_0_
  15.7 8.5 %collective-permute-start.5 = (bf16[192,1152]{1,0:T(8,128)(2,1)S(1)}, bf16[192,1152]{1,0:T(8,128)(2,1)S(1)}, u32[]{:S(2)}, u32[]{:S(2)}) collective-permute-start(bf16[192,1152]{1,0:T(8,128)(2,1)S(1)} %get-tuple-element.30), channel_id=1, source_target_pairs={{0,4},{4,0},{8,12},{12,8},{16,20},{20,16},{24,28},{28,24},{1,5},{5... | collective-permute-start | bytes 1327112 | tf_op jit(solution)/shard_map/ppermute | solution.py:23
  24.2 1.0 %more.4.dir_ref = f32[2,192,1152]{2,1,0:T(8,128)S(1)} custom-call(f32[8,128]{1,0:T(8,128)S(1)} %get-tuple-element.18.scale_ref, bf16[2,192,1152]{2,1,0:T(8,128)(2,1)S(1)} %get-tuple-element.19.half_ref, f32[2,192,1152]{2,1,0:T(8,128)S(1)} %get-tuple-element.23.dir_ref, ...), custom_call_target="tpu_custom_call", output_to_operand_aliasing={{}: (2, {})} | custom-call | flops 1000 | bytes 1000 | tf_op jit(solution)/shard_map/more/pallas_call | solution.py:290
  25.1 1.0 %collective-permute-done.2.raw_ref = bf16[192,1152]{1,0:T(8,128)(2,1)S(1)} collective-permute-done((bf16[192,1152]{1,0:T(8,128)(2,1)S(1)}, bf16[192,1152]{1,0:T(8,128)(2,1)S(1)}, u32[]{:S(2)}, u32[]{:S(2)}) %collective-permute-start.2) | collective-permute-done | bytes 442400 | tf_op jit(solution)/shard_map/ppermute | solution.py:23
  26.1 0.2 unit.1.rest_2_
  26.3 0.0 collective-permute-done.rest_0_
  26.3 0.0 collective-permute-done.1.rest_1_
  26.3 0.9 %collective-permute-start.7 = (bf16[192,1152]{1,0:T(8,128)(2,1)S(1)}, bf16[192,1152]{1,0:T(8,128)(2,1)S(1)}, u32[]{:S(2)}, u32[]{:S(2)}) collective-permute-start(bf16[192,1152]{1,0:T(8,128)(2,1)S(1)} %collective-permute-done.rest_0_), channel_id=1, source_target_pairs={{0,4},{4,0},{8,12},{12,8},{16,20},{20,16},{24,28},{28,24},{1,5},{5... | collective-permute-start | bytes 1327112 | tf_op jit(solution)/shard_map/ppermute | solution.py:23
  27.3 0.0 collective-permute-done.6.rest_4_
  27.3 0.0 collective-permute-done.5.rest_3_
  27.3 2.0 %more.5.dir_ref = f32[2,192,1152]{2,1,0:T(8,128)S(1)} custom-call(f32[8,128]{1,0:T(8,128)S(1)} %get-tuple-element.18.scale_ref, bf16[2,192,1152]{2,1,0:T(8,128)(2,1)S(1)} %get-tuple-element.19.half_ref, f32[2,192,1152]{2,1,0:T(8,128)S(1)} %more.4.dir_ref, bf16[192,1152]{1,0:T(8,128)(2,1)S(1)} %collective-permute-done.rest_0_, ...), custom_call_target="tpu_custom_call", output_to_operand_aliasing={{}: (2, {})} | custom-call | flops 4000000 | bytes 4000000 | tf_op jit(solution)/shard_map/more/pallas_call | solution.py:290
  29.3 0.0 collective-permute-done.7.rest_0_
  29.3 2.0 %last.1 = (f32[192,1152]{1,0:T(8,128)}, f32[192,1152]{1,0:T(8,128)}) custom-call(f32[8,128]{1,0:T(8,128)S(1)} %get-tuple-element.18.scale_ref, bf16[2,192,1152]{2,1,0:T(8,128)(2,1)S(1)} %get-tuple-element.19.half_ref, f32[2,192,1152]{2,1,0:T(8,128)S(1)} %more.5.dir_ref, bf16[2,192,1152]{2,1,0:T(8,128)(2,1)S(1)} %get-tuple-element.32.raw_ref, ...), custom_call_target="tpu_custom_call" | custom-call | flops 1000 | bytes 1000 | tf_op jit(solution)/shard_map/last/pallas_call | solution.py:315
Async XLA Ops:
  0.6 12.6 %collective-permute-start.3 = (bf16[192,1152]{1,0:T(8,128)(2,1)}, bf16[192,1152]{1,0:T(8,128)(2,1)S(1)}, u32[]{:S(2)}, u32[]{:S(2)}) collective-permute-start(bf16[192,1152]{1,0:T(8,128)(2,1)} %txt_ref.3), channel_id=1, source_target_pairs={{0,8},{4,12},{8,16},{12,20},{16,24},{20,28},{24,0},{28,4},{1,9},{5... | collective-permute-start | bytes 1327112 | tf_op jit(solution)/shard_map/ppermute | solution.py:23
  1.9 13.8 %collective-permute-start.4 = (bf16[192,1152]{1,0:T(8,128)(2,1)}, bf16[192,1152]{1,0:T(8,128)(2,1)S(1)}, u32[]{:S(2)}, u32[]{:S(2)}) collective-permute-start(bf16[192,1152]{1,0:T(8,128)(2,1)} %txt_ref.3), channel_id=1, source_target_pairs={{0,1},{1,2},{2,3},{3,0},{4,5},{5,6},{6,7},{7,4},{8,9},{9,10},{10,1... | collective-permute-start | bytes 1327112 | tf_op jit(solution)/shard_map/ppermute | solution.py:23
  4.3 21.8 %collective-permute-start.2 = (bf16[192,1152]{1,0:T(8,128)(2,1)S(1)}, bf16[192,1152]{1,0:T(8,128)(2,1)S(1)}, u32[]{:S(2)}, u32[]{:S(2)}) collective-permute-start(bf16[192,1152]{1,0:T(8,128)(2,1)S(1)} %pick.1), channel_id=1, source_target_pairs={{0,20},{4,16},{8,28},{12,24},{16,4},{20,0},{24,12},{28,8},{1,21},{... | collective-permute-start | bytes 1327112 | tf_op jit(solution)/shard_map/ppermute | solution.py:23
  7.1 19.2 %collective-permute-start = (bf16[192,1152]{1,0:T(8,128)(2,1)S(1)}, bf16[192,1152]{1,0:T(8,128)(2,1)S(1)}, u32[]{:S(2)}, u32[]{:S(2)}) collective-permute-start(bf16[192,1152]{1,0:T(8,128)(2,1)S(1)} %norm.1.img_half), channel_id=1, source_target_pairs={{0,24},{4,28},{8,0},{12,4},{16,8},{20,12},{24,16},{28,20},{1,25},{... | collective-permute-start | bytes 1327112 | tf_op jit(solution)/shard_map/ppermute | solution.py:23
  8.4 17.9 %collective-permute-start.1 = (bf16[192,1152]{1,0:T(8,128)(2,1)S(1)}, bf16[192,1152]{1,0:T(8,128)(2,1)S(1)}, u32[]{:S(2)}, u32[]{:S(2)}) collective-permute-start(bf16[192,1152]{1,0:T(8,128)(2,1)S(1)} %norm.1.img_half), channel_id=1, source_target_pairs={{0,3},{1,0},{2,1},{3,2},{4,7},{5,4},{6,5},{7,6},{8,11},{9,8},{10,9... | collective-permute-start | bytes 1327112 | tf_op jit(solution)/shard_map/ppermute | solution.py:23
  14.2 13.0 %collective-permute-start.6 = (bf16[192,1152]{1,0:T(8,128)(2,1)S(1)}, bf16[192,1152]{1,0:T(8,128)(2,1)S(1)}, u32[]{:S(2)}, u32[]{:S(2)}) collective-permute-start(bf16[192,1152]{1,0:T(8,128)(2,1)S(1)} %get-tuple-element.31), channel_id=1, source_target_pairs={{0,4},{4,0},{8,12},{12,8},{16,20},{20,16},{24,28},{28,24},{1,5},{5... | collective-permute-start | bytes 1327112 | tf_op jit(solution)/shard_map/ppermute | solution.py:23
  15.7 11.6 %collective-permute-start.5 = (bf16[192,1152]{1,0:T(8,128)(2,1)S(1)}, bf16[192,1152]{1,0:T(8,128)(2,1)S(1)}, u32[]{:S(2)}, u32[]{:S(2)}) collective-permute-start(bf16[192,1152]{1,0:T(8,128)(2,1)S(1)} %get-tuple-element.30), channel_id=1, source_target_pairs={{0,4},{4,0},{8,12},{12,8},{16,20},{20,16},{24,28},{28,24},{1,5},{5... | collective-permute-start | bytes 1327112 | tf_op jit(solution)/shard_map/ppermute | solution.py:23
  26.3 3.0 %collective-permute-start.7 = (bf16[192,1152]{1,0:T(8,128)(2,1)S(1)}, bf16[192,1152]{1,0:T(8,128)(2,1)S(1)}, u32[]{:S(2)}, u32[]{:S(2)}) collective-permute-start(bf16[192,1152]{1,0:T(8,128)(2,1)S(1)} %collective-permute-done.rest_0_), channel_id=1, source_target_pairs={{0,4},{4,0},{8,12},{12,8},{16,20},{20,16},{24,28},{28,24},{1,5},{5... | collective-permute-start | bytes 1327112 | tf_op jit(solution)/shard_map/ppermute | solution.py:23

commit v4 on v3

--- a/solution.py
+++ b/solution.py
@@ -216,8 +216,7 @@
     return kinds, jax.tree.leaves([block for _, block in entries])
 
 
-def visit_all(kinds, blocks, scale_ref, half_ref, dir_ref, acc_ref, others_ref, sides=(0, 1)):
-    rows = half_ref.shape[1]
+def place_all(kinds, blocks, rows, others_ref):
     blocks = parts_of(kinds, blocks, rows)
     pairs = sum(side == 2 for side, _ in kinds)
     counts = [sum(kind[0] == side for kind in kinds) + pairs for side in (0, 1)]
@@ -236,12 +235,22 @@
             at = start if isinstance(start, int) else pl.multiple_of(start, 16)
             others_ref[pl.ds(at, size)] = unit_half(part[...]) if raw else part[...]
             start += size
-    for side in sides:
-        if counts[side]:
-            others = others_ref[pl.ds(side * counts[0] * rows, counts[side] * rows)]
-            acc_ref[side] = dir_ref[side] + visit(half_ref[side], others, scale_ref)
-        else:
-            acc_ref[side] = dir_ref[side]
+    return counts
+
+
+def visit_side(side, counts, scale_ref, half_ref, dir_ref, acc_ref, others_ref):
+    rows = half_ref.shape[1]
+    if counts[side]:
+        others = others_ref[pl.ds(side * counts[0] * rows, counts[side] * rows)]
+        acc_ref[side] = dir_ref[side] + visit(half_ref[side], others, scale_ref)
+    else:
+        acc_ref[side] = dir_ref[side]
+
+
+def visit_all(kinds, blocks, scale_ref, half_ref, dir_ref, acc_ref, others_ref):
+    counts = place_all(kinds, blocks, half_ref.shape[1], others_ref)
+    for side in (0, 1):
+        visit_side(side, counts, scale_ref, half_ref, dir_ref, acc_ref, others_ref)
 
 
 def more_kernel(kinds, given, scale_ref, half_ref, dir_ref, *rest):
@@ -264,21 +273,25 @@
     return copies
 
 
-def last_kernel(kinds, scale_ref, half_ref, dir_ref, raw_ref, inverse_ref, *rest):
-    blocks, (img_grad, txt_grad, acc_ref, others_ref, held_ref, sems) = rest[:-6], rest[-6:]
-    texts = any(side == 0 for side, _ in kinds)
-    if texts:
-        visit_all(kinds, blocks, scale_ref, half_ref, dir_ref, acc_ref, others_ref)
-    source = acc_ref if texts else dir_ref
+def image_kernel(kinds, scale_ref, half_ref, dir_ref, raw_ref, inverse_ref, *rest):
+    blocks, (out_ref, img_grad, others_ref, held_ref, sems) = rest[:-5], rest[-5:]
+    counts = place_all(kinds, blocks, half_ref.shape[1], others_ref)
+    visit_side(0, counts, scale_ref, half_ref, dir_ref, out_ref, others_ref)
     copies = finish(
-        raw_ref.at[0], inverse_ref.at[0], source.at[0], img_grad, held_ref.at[0], sems.at[0]
-    )
-    if not texts:
-        visit_all(kinds, blocks, scale_ref, half_ref, dir_ref, acc_ref, others_ref, (1,))
-    copies += finish(
-        raw_ref.at[1], inverse_ref.at[1], acc_ref.at[1], txt_grad, held_ref.at[1], sems.at[1]
-    )
+        raw_ref.at[0], inverse_ref.at[0], out_ref.at[0], img_grad, held_ref, sems
+    )
+    visit_side(1, counts, scale_ref, half_ref, dir_ref, out_ref, others_ref)
     for copy in copies:
+        copy.wait()
+
+
+def text_kernel(kinds, scale_ref, half_ref, dir_ref, raw_ref, inverse_ref, *rest):
+    blocks, (txt_grad, acc_ref, others_ref, held_ref, sems) = rest[:-5], rest[-5:]
+    counts = place_all(kinds, blocks, half_ref.shape[1], others_ref)
+    visit_side(1, counts, scale_ref, half_ref, dir_ref, acc_ref, others_ref)
+    for copy in finish(
+        raw_ref.at[1], inverse_ref.at[1], acc_ref.at[1], txt_grad, held_ref, sems
+    ):
         copy.wait()
 
 
@@ -308,22 +321,26 @@
     return call(unit_kernel, jax.ShapeDtypeStruct(raw.shape, raw.dtype), [VMEM], VMEM, name="unit")(raw)
 
 
-def last_visits(scale, half, direction, raw, inverse, entries):
+def grad_visits(kernel, scale, half, direction, raw, inverse, entries, work=1000):
     kinds, blocks = flat(entries)
     rows, width = half.shape[1:]
+    sums = jax.ShapeDtypeStruct(direction.shape, direction.dtype)
     grad = jax.ShapeDtypeStruct((rows, width), jnp.float32)
+    scratch = [
+        pltpu.VMEM((max(1, len(kinds)) * rows, width), jnp.bfloat16),
+        pltpu.VMEM(grad.shape, grad.dtype),
+        pltpu.SemaphoreType.DMA((len(pieces(rows)),)),
+    ]
+    image = kernel is image_kernel
     return call(
-        functools.partial(last_kernel, kinds),
-        (grad, grad),
+        functools.partial(kernel, kinds),
+        (sums, grad) if image else grad,
         [VMEM] * (5 + len(blocks)),
-        (HBM, HBM),
-        scratch_shapes=[
-            pltpu.VMEM(direction.shape, direction.dtype),
-            pltpu.VMEM((max(1, len(kinds)) * rows, width), jnp.bfloat16),
-            pltpu.VMEM(direction.shape, direction.dtype),
-            pltpu.SemaphoreType.DMA((2, len(pieces(rows)))),
-        ],
-        name="last",
+        (VMEM, HBM) if image else HBM,
+        work=work,
+        scratch_shapes=scratch if image else [pltpu.VMEM(sums.shape, sums.dtype)] + scratch,
+        input_output_aliases={2: 0} if image else {},
+        name="image" if image else "text",
     )(scale, half, direction, raw, inverse, *blocks)
 
 
@@ -354,8 +371,11 @@
         for k in range(1, row_extent):
             text_rows.append(((0, True), along(txt, "row", lambda s: s + k)))
             image_rows.append(((1, False), along(img_half, "row", lambda s: s - k)))
-        last = text_cols + image_cols + text_rows + image_rows
-        return last_visits(scale, half, direction, raw, inverse, last)
+        entries = text_cols + image_cols + text_rows + image_rows
+        direction, image_grad = grad_visits(
+            image_kernel, scale, half, direction, raw, inverse, entries
+        )
+        return image_grad, grad_visits(text_kernel, scale, half, direction, raw, inverse, [])
 
     reach = row_extent - 1
     far = along(pick(*held), "row", lambda s: s + reach if s % 2 else s - reach)
@@ -376,8 +396,10 @@
     middle = image_rows + image_cols + [((2, False), normalized(far))]
     middle, direction = tied(middle, direction)
     last = [(kind, along(block, "row", swap)) for kind, block in middle[: len(image_rows)]]
-    direction = more_visits(scale, half, direction, middle + swapped, work=4000000)
-    return last_visits(scale, half, direction, raw, inverse, last)
+    direction, image_grad = grad_visits(
+        image_kernel, scale, half, direction, raw, inverse, middle + swapped, work=4000000
+    )
+    return image_grad, grad_visits(text_kernel, scale, half, direction, raw, inverse, last)
 
 
 def solution(mesh):

time: 31.5 us -> 31.6 us (level)
    pallas_call x1 -> x2, Pallas kernels: 2.01 us -> 4.14 us  [grad_visits(): call(functools.partial(kernel, kinds), (sums, grad) if image else grad, [...]
    pallas_call x3 -> x2, Pallas kernels: 3.98 us -> 1.98 us  [more_visits(): call(functools.partial(more_kernel, kinds, len(halves)), (jax.ShapeDtypeS...]
  transfers between devices with their start and end apart: 8 -> 8, of which waited for: 1 -> 1; matrix products, arithmetic and copies ran while one was open for 0% -> 0% of each run, Pallas kernels for 32% -> 33%
where the time goes in v4:
time: 31.6 us; the launch traced here: 31.4 us
  starting transfers between devices  16.4 us (52%)
  Pallas kernels  12.1 us (38%)
  between operations  2.01 us (6%)
  waiting for transfers between devices  0.98 us (3%)
    ppermute x8, starting transfers between devices, along(): return lax.ppermute(value, axis, pairs)  16.4 us
    pallas_call x2, Pallas kernels, grad_visits(): call(functools.partial(kernel, kinds), (sums, grad) if image else grad, [...  4.14 us
    pallas_call x1, Pallas kernels, own_visit(): call(own_kernel, (jax.ShapeDtypeStruct((8, 128), jnp.float32), both, both...  3.31 us
    pallas_call x2, Pallas kernels, more_visits(): call(functools.partial(more_kernel, kinds, len(halves)), (jax.ShapeDtypeS...  1.98 us
    pallas_call x1, Pallas kernels, norm(): call(norm_kernel, one, [HBM], VMEM, scratch_shapes=[pltpu.VMEM(img.shape,...  1.38 us
    pallas_call x1, Pallas kernels, pick(): call(pick_kernel, jax.ShapeDtypeStruct(img.shape, img.dtype), [HBM, HBM],...  1.09 us
    ppermute x8, waiting for transfers between devices, along(): return lax.ppermute(value, axis, pairs)  0.98 us
  transfers between devices with their start and end apart: 8, of which 1 were waited for; matrix products, arithmetic and copies ran while one was open for 0% of the time, Pallas kernels for 33%

profile of v4, /device:TPU:19, one launch (start us, length us, event | category | flops | bytes accessed | tf_op | source)
XLA Modules:
  0.0 31.4 jit_solution(1531091057405384566)
XLA Ops:
  0.6 1.3 %collective-permute-start.3 = (bf16[192,1152]{1,0:T(8,128)(2,1)}, bf16[192,1152]{1,0:T(8,128)(2,1)S(1)}, u32[]{:S(2)}, u32[]{:S(2)}) collective-permute-start(bf16[192,1152]{1,0:T(8,128)(2,1)} %txt_ref.3), channel_id=1, source_target_pairs={{0,8},{4,12},{8,16},{12,20},{16,24},{20,28},{24,0},{28,4},{1,9},{5... | collective-permute-start | bytes 1327112 | tf_op jit(solution)/shard_map/ppermute | solution.py:23
  1.9 1.3 %collective-permute-start.4 = (bf16[192,1152]{1,0:T(8,128)(2,1)}, bf16[192,1152]{1,0:T(8,128)(2,1)S(1)}, u32[]{:S(2)}, u32[]{:S(2)}) collective-permute-start(bf16[192,1152]{1,0:T(8,128)(2,1)} %txt_ref.3), channel_id=1, source_target_pairs={{0,1},{1,2},{2,3},{3,0},{4,5},{5,6},{6,7},{7,4},{8,9},{9,10},{10,1... | collective-permute-start | bytes 1327112 | tf_op jit(solution)/shard_map/ppermute | solution.py:23
  3.2 1.1 %pick.1 = bf16[192,1152]{1,0:T(8,128)(2,1)S(1)} custom-call(bf16[192,1152]{1,0:T(8,128)(2,1)} %img_ref.5, bf16[192,1152]{1,0:T(8,128)(2,1)} %txt_ref.3), custom_call_target="tpu_custom_call" | custom-call | flops 1000 | bytes 1000 | tf_op jit(solution)/shard_map/pick/pallas_call | solution.py:110
  4.3 1.4 %collective-permute-start.2 = (bf16[192,1152]{1,0:T(8,128)(2,1)S(1)}, bf16[192,1152]{1,0:T(8,128)(2,1)S(1)}, u32[]{:S(2)}, u32[]{:S(2)}) collective-permute-start(bf16[192,1152]{1,0:T(8,128)(2,1)S(1)} %pick.1), channel_id=1, source_target_pairs={{0,20},{4,16},{8,28},{12,24},{16,4},{20,0},{24,12},{28,8},{1,21},{... | collective-permute-start | bytes 1327112 | tf_op jit(solution)/shard_map/ppermute | solution.py:23
  5.7 1.4 %norm.1.img_half = bf16[192,1152]{1,0:T(8,128)(2,1)S(1)} custom-call(bf16[192,1152]{1,0:T(8,128)(2,1)} %img_ref.5), custom_call_target="tpu_custom_call" | custom-call | flops 1000 | bytes 1000 | tf_op jit(solution)/shard_map/norm/pallas_call | solution.py:141
  7.1 1.3 %collective-permute-start = (bf16[192,1152]{1,0:T(8,128)(2,1)S(1)}, bf16[192,1152]{1,0:T(8,128)(2,1)S(1)}, u32[]{:S(2)}, u32[]{:S(2)}) collective-permute-start(bf16[192,1152]{1,0:T(8,128)(2,1)S(1)} %norm.1.img_half), channel_id=1, source_target_pairs={{0,24},{4,28},{8,0},{12,4},{16,8},{20,12},{24,16},{28,20},{1,25},{... | collective-permute-start | bytes 1327112 | tf_op jit(solution)/shard_map/ppermute | solution.py:23
  8.4 0.2 collective-permute-start.1
  9.9 3.3 %own.1 = (f32[8,128]{1,0:T(8,128)S(1)}, bf16[2,192,1152]{2,1,0:T(8,128)(2,1)S(1)}, bf16[2,192,1152]{2,1,0:T(8,128)(2,1)S(1)}, f32[2,192,128]{2,1,0:T(8,128)S(1)}...) custom-call(f32[1,1]{1,0:T(1,128)} %bitcast.2.exponent_ref, f32[1,1]{1,0:T(1,128)} %bitcast.3.offset_ref, ...), custom_call_target="tpu_custom_call" | custom-call | flops 1000 | bytes 1000 | tf_op jit(solution)/shard_map/own/pallas_call | solution.py:187
  13.2 0.0 collective-permute-done.3.rest_0_
  13.2 1.0 %more.2 = (f32[2,192,1152]{2,1,0:T(8,128)S(1)}, bf16[192,1152]{1,0:T(8,128)(2,1)S(1)}) custom-call(f32[8,128]{1,0:T(8,128)S(1)} %get-tuple-element.20.scale_ref, bf16[2,192,1152]{2,1,0:T(8,128)(2,1)S(1)} %get-tuple-element.21.half_ref, f32[2,192,1152]{2,1,0:T(8,128)S(1)} %get-tuple-element.23.dir_ref, ...), custom_call_target="tpu_custom_call", output_to_operand_aliasing={{0}: (2, {})} | custom-call | flops 1000 | bytes 1000 | tf_op jit(solution)/shard_map/more/pallas_call | solution.py:303
  14.2 1.5 %collective-permute-start.6 = (bf16[192,1152]{1,0:T(8,128)(2,1)S(1)}, bf16[192,1152]{1,0:T(8,128)(2,1)S(1)}, u32[]{:S(2)}, u32[]{:S(2)}) collective-permute-start(bf16[192,1152]{1,0:T(8,128)(2,1)S(1)} %get-tuple-element.35), channel_id=1, source_target_pairs={{0,4},{4,0},{8,12},{12,8},{16,20},{20,16},{24,28},{28,24},{1,5},{5... | collective-permute-start | bytes 1327112 | tf_op jit(solution)/shard_map/ppermute | solution.py:23
  15.7 0.0 collective-permute-done.4.rest_0_
  15.7 8.5 %collective-permute-start.5 = (bf16[192,1152]{1,0:T(8,128)(2,1)S(1)}, bf16[192,1152]{1,0:T(8,128)(2,1)S(1)}, u32[]{:S(2)}, u32[]{:S(2)}) collective-permute-start(bf16[192,1152]{1,0:T(8,128)(2,1)S(1)} %get-tuple-element.34), channel_id=1, source_target_pairs={{0,4},{4,0},{8,12},{12,8},{16,20},{20,16},{24,28},{28,24},{1,5},{5... | collective-permute-start | bytes 1327112 | tf_op jit(solution)/shard_map/ppermute | solution.py:23
  24.2 1.0 %more.3.dir_ref = f32[2,192,1152]{2,1,0:T(8,128)S(1)} custom-call(f32[8,128]{1,0:T(8,128)S(1)} %get-tuple-element.20.scale_ref, bf16[2,192,1152]{2,1,0:T(8,128)(2,1)S(1)} %get-tuple-element.21.half_ref, f32[2,192,1152]{2,1,0:T(8,128)S(1)} %get-tuple-element.25.dir_ref, ...), custom_call_target="tpu_custom_call", output_to_operand_aliasing={{}: (2, {})} | custom-call | flops 1000 | bytes 1000 | tf_op jit(solution)/shard_map/more/pallas_call | solution.py:303
  25.1 1.0 %collective-permute-done.2.raw_ref = bf16[192,1152]{1,0:T(8,128)(2,1)S(1)} collective-permute-done((bf16[192,1152]{1,0:T(8,128)(2,1)S(1)}, bf16[192,1152]{1,0:T(8,128)(2,1)S(1)}, u32[]{:S(2)}, u32[]{:S(2)}) %collective-permute-start.2) | collective-permute-done | bytes 442400 | tf_op jit(solution)/shard_map/ppermute | solution.py:23
  26.1 0.2 unit.1.rest_2_
  26.3 0.0 collective-permute-done.rest_0_
  26.3 0.0 collective-permute-done.1.rest_1_
  26.3 0.9 %collective-permute-start.7 = (bf16[192,1152]{1,0:T(8,128)(2,1)S(1)}, bf16[192,1152]{1,0:T(8,128)(2,1)S(1)}, u32[]{:S(2)}, u32[]{:S(2)}) collective-permute-start(bf16[192,1152]{1,0:T(8,128)(2,1)S(1)} %collective-permute-done.rest_0_), channel_id=1, source_target_pairs={{0,4},{4,0},{8,12},{12,8},{16,20},{20,16},{24,28},{28,24},{1,5},{5... | collective-permute-start | bytes 1327112 | tf_op jit(solution)/shard_map/ppermute | solution.py:23
  27.3 0.0 collective-permute-done.6.rest_4_
  27.3 0.0 collective-permute-done.5.rest_3_
  27.3 2.3 %image.1 = (f32[2,192,1152]{2,1,0:T(8,128)S(1)}, f32[192,1152]{1,0:T(8,128)}) custom-call(f32[8,128]{1,0:T(8,128)S(1)} %get-tuple-element.20.scale_ref, bf16[2,192,1152]{2,1,0:T(8,128)(2,1)S(1)} %get-tuple-element.21.half_ref, f32[2,192,1152]{2,1,0:T(8,128)S(1)} %more.3.dir_ref, ...), custom_call_target="tpu_custom_call", output_to_operand_aliasing={{0}: (2, {})} | custom-call | flops 4000000 | bytes 4000000 | tf_op jit(solution)/shard_map/image/pallas_call | solution.py:335
  29.5 0.0 collective-permute-done.7.rest_0_
  29.6 1.9 %text.1 = f32[192,1152]{1,0:T(8,128)} custom-call(f32[8,128]{1,0:T(8,128)S(1)} %get-tuple-element.20.scale_ref, bf16[2,192,1152]{2,1,0:T(8,128)(2,1)S(1)} %get-tuple-element.21.half_ref, f32[2,192,1152]{2,1,0:T(8,128)S(1)} %get-tuple-element.37.dir_ref, bf16[2,192,1152]{2,1,0:T(8,128)(2,1)S(1)} %get-tuple-element.29.raw_ref, ...), custom_call_target="tpu_custom_call" | custom-call | flops 1000 | bytes 1000 | tf_op jit(solution)/shard_map/text/pallas_call | solution.py:335
Async XLA Ops:
  0.6 12.6 %collective-permute-start.3 = (bf16[192,1152]{1,0:T(8,128)(2,1)}, bf16[192,1152]{1,0:T(8,128)(2,1)S(1)}, u32[]{:S(2)}, u32[]{:S(2)}) collective-permute-start(bf16[192,1152]{1,0:T(8,128)(2,1)} %txt_ref.3), channel_id=1, source_target_pairs={{0,8},{4,12},{8,16},{12,20},{16,24},{20,28},{24,0},{28,4},{1,9},{5... | collective-permute-start | bytes 1327112 | tf_op jit(solution)/shard_map/ppermute | solution.py:23
  1.9 13.8 %collective-permute-start.4 = (bf16[192,1152]{1,0:T(8,128)(2,1)}, bf16[192,1152]{1,0:T(8,128)(2,1)S(1)}, u32[]{:S(2)}, u32[]{:S(2)}) collective-permute-start(bf16[192,1152]{1,0:T(8,128)(2,1)} %txt_ref.3), channel_id=1, source_target_pairs={{0,1},{1,2},{2,3},{3,0},{4,5},{5,6},{6,7},{7,4},{8,9},{9,10},{10,1... | collective-permute-start | bytes 1327112 | tf_op jit(solution)/shard_map/ppermute | solution.py:23
  4.3 21.8 %collective-permute-start.2 = (bf16[192,1152]{1,0:T(8,128)(2,1)S(1)}, bf16[192,1152]{1,0:T(8,128)(2,1)S(1)}, u32[]{:S(2)}, u32[]{:S(2)}) collective-permute-start(bf16[192,1152]{1,0:T(8,128)(2,1)S(1)} %pick.1), channel_id=1, source_target_pairs={{0,20},{4,16},{8,28},{12,24},{16,4},{20,0},{24,12},{28,8},{1,21},{... | collective-permute-start | bytes 1327112 | tf_op jit(solution)/shard_map/ppermute | solution.py:23
  7.1 19.2 %collective-permute-start = (bf16[192,1152]{1,0:T(8,128)(2,1)S(1)}, bf16[192,1152]{1,0:T(8,128)(2,1)S(1)}, u32[]{:S(2)}, u32[]{:S(2)}) collective-permute-start(bf16[192,1152]{1,0:T(8,128)(2,1)S(1)} %norm.1.img_half), channel_id=1, source_target_pairs={{0,24},{4,28},{8,0},{12,4},{16,8},{20,12},{24,16},{28,20},{1,25},{... | collective-permute-start | bytes 1327112 | tf_op jit(solution)/shard_map/ppermute | solution.py:23
  8.4 17.9 %collective-permute-start.1 = (bf16[192,1152]{1,0:T(8,128)(2,1)S(1)}, bf16[192,1152]{1,0:T(8,128)(2,1)S(1)}, u32[]{:S(2)}, u32[]{:S(2)}) collective-permute-start(bf16[192,1152]{1,0:T(8,128)(2,1)S(1)} %norm.1.img_half), channel_id=1, source_target_pairs={{0,3},{1,0},{2,1},{3,2},{4,7},{5,4},{6,5},{7,6},{8,11},{9,8},{10,9... | collective-permute-start | bytes 1327112 | tf_op jit(solution)/shard_map/ppermute | solution.py:23
  14.2 13.0 %collective-permute-start.6 = (bf16[192,1152]{1,0:T(8,128)(2,1)S(1)}, bf16[192,1152]{1,0:T(8,128)(2,1)S(1)}, u32[]{:S(2)}, u32[]{:S(2)}) collective-permute-start(bf16[192,1152]{1,0:T(8,128)(2,1)S(1)} %get-tuple-element.35), channel_id=1, source_target_pairs={{0,4},{4,0},{8,12},{12,8},{16,20},{20,16},{24,28},{28,24},{1,5},{5... | collective-permute-start | bytes 1327112 | tf_op jit(solution)/shard_map/ppermute | solution.py:23
  15.7 11.6 %collective-permute-start.5 = (bf16[192,1152]{1,0:T(8,128)(2,1)S(1)}, bf16[192,1152]{1,0:T(8,128)(2,1)S(1)}, u32[]{:S(2)}, u32[]{:S(2)}) collective-permute-start(bf16[192,1152]{1,0:T(8,128)(2,1)S(1)} %get-tuple-element.34), channel_id=1, source_target_pairs={{0,4},{4,0},{8,12},{12,8},{16,20},{20,16},{24,28},{28,24},{1,5},{5... | collective-permute-start | bytes 1327112 | tf_op jit(solution)/shard_map/ppermute | solution.py:23
  26.3 3.2 %collective-permute-start.7 = (bf16[192,1152]{1,0:T(8,128)(2,1)S(1)}, bf16[192,1152]{1,0:T(8,128)(2,1)S(1)}, u32[]{:S(2)}, u32[]{:S(2)}) collective-permute-start(bf16[192,1152]{1,0:T(8,128)(2,1)S(1)} %collective-permute-done.rest_0_), channel_id=1, source_target_pairs={{0,4},{4,0},{8,12},{12,8},{16,20},{20,16},{24,28},{28,24},{1,5},{5... | collective-permute-start | bytes 1327112 | tf_op jit(solution)/shard_map/ppermute | solution.py:23

commit v5 on v4

--- a/solution.py
+++ b/solution.py
@@ -393,11 +393,10 @@
     if text_cols:
         direction = more_visits(scale, half, direction, text_cols)
     far, direction = lax.optimization_barrier((far, direction))
+    last = [(kind, along(block, "row", swap)) for kind, block in image_rows]
     middle = image_rows + image_cols + [((2, False), normalized(far))]
-    middle, direction = tied(middle, direction)
-    last = [(kind, along(block, "row", swap)) for kind, block in middle[: len(image_rows)]]
     direction, image_grad = grad_visits(
-        image_kernel, scale, half, direction, raw, inverse, middle + swapped, work=4000000
+        image_kernel, scale, half, direction, raw, inverse, middle + swapped, work=100000000
     )
     return image_grad, grad_visits(text_kernel, scale, half, direction, raw, inverse, last)
 

time: 31.6 us -> 35.9 us (1.14)
  the two profiles are of different devices: /device:TPU:19 before, /device:TPU:3 now
where the time goes in v5:
time: 35.9 us; the launch traced here: 35.7 us
  Pallas kernels  12.1 us (34%)
  starting transfers between devices  10.8 us (30%)
  waiting for transfers between devices  10.7 us (30%)
  between operations  2.03 us (6%)
    ppermute x8, starting transfers between devices, along(): return lax.ppermute(value, axis, pairs)  10.8 us
    ppermute x8, waiting for transfers between devices, along(): return lax.ppermute(value, axis, pairs)  10.7 us
    pallas_call x2, Pallas kernels, grad_visits(): call(functools.partial(kernel, kinds), (sums, grad) if image else grad, [...  4.14 us
    pallas_call x1, Pallas kernels, own_visit(): call(own_kernel, (jax.ShapeDtypeStruct((8, 128), jnp.float32), both, both...  3.31 us
    pallas_call x2, Pallas kernels, more_visits(): call(functools.partial(more_kernel, kinds, len(halves)), (jax.ShapeDtypeS...  1.98 us
    pallas_call x1, Pallas kernels, norm(): call(norm_kernel, one, [HBM], VMEM, scratch_shapes=[pltpu.VMEM(img.shape,...  1.38 us
    pallas_call x1, Pallas kernels, pick(): call(pick_kernel, jax.ShapeDtypeStruct(img.shape, img.dtype), [HBM, HBM],...  1.09 us
  transfers between devices with their start and end apart: 8, of which 2 were waited for; matrix products, arithmetic and copies ran while one was open for 0% of the time, Pallas kernels for 29%

profile of v5, /device:TPU:3, one launch (start us, length us, event | category | flops | bytes accessed | tf_op | source)
XLA Modules:
  0.0 35.7 jit_solution(16619252756682963646)
XLA Ops:
  0.6 1.3 %collective-permute-start.1 = (bf16[192,1152]{1,0:T(8,128)(2,1)}, bf16[192,1152]{1,0:T(8,128)(2,1)S(1)}, u32[]{:S(2)}, u32[]{:S(2)}) collective-permute-start(bf16[192,1152]{1,0:T(8,128)(2,1)} %txt_ref.3), channel_id=1, source_target_pairs={{0,8},{4,12},{8,16},{12,20},{16,24},{20,28},{24,0},{28,4},{1,9},{5... | collective-permute-start | bytes 1327112 | tf_op jit(solution)/shard_map/ppermute | solution.py:23
  1.9 1.3 %collective-permute-start.2 = (bf16[192,1152]{1,0:T(8,128)(2,1)}, bf16[192,1152]{1,0:T(8,128)(2,1)S(1)}, u32[]{:S(2)}, u32[]{:S(2)}) collective-permute-start(bf16[192,1152]{1,0:T(8,128)(2,1)} %txt_ref.3), channel_id=1, source_target_pairs={{0,1},{1,2},{2,3},{3,0},{4,5},{5,6},{6,7},{7,4},{8,9},{9,10},{10,1... | collective-permute-start | bytes 1327112 | tf_op jit(solution)/shard_map/ppermute | solution.py:23
  3.2 1.4 %norm.1.img_half = bf16[192,1152]{1,0:T(8,128)(2,1)S(1)} custom-call(bf16[192,1152]{1,0:T(8,128)(2,1)} %img_ref.5), custom_call_target="tpu_custom_call" | custom-call | flops 1000 | bytes 1000 | tf_op jit(solution)/shard_map/norm/pallas_call | solution.py:141
  4.6 0.3 collective-permute-start.3
  4.9 2.0 %collective-permute-start.4 = (bf16[192,1152]{1,0:T(8,128)(2,1)S(1)}, bf16[192,1152]{1,0:T(8,128)(2,1)S(1)}, u32[]{:S(2)}, u32[]{:S(2)}) collective-permute-start(bf16[192,1152]{1,0:T(8,128)(2,1)S(1)} %norm.1.img_half), channel_id=1, source_target_pairs={{0,3},{1,0},{2,1},{3,2},{4,7},{5,4},{6,5},{7,6},{8,11},{9,8},{10,9... | collective-permute-start | bytes 1327112 | tf_op jit(solution)/shard_map/ppermute | solution.py:23
  6.9 1.1 %pick.1 = bf16[192,1152]{1,0:T(8,128)(2,1)S(1)} custom-call(bf16[192,1152]{1,0:T(8,128)(2,1)} %img_ref.5, bf16[192,1152]{1,0:T(8,128)(2,1)} %txt_ref.3), custom_call_target="tpu_custom_call" | custom-call | flops 1000 | bytes 1000 | tf_op jit(solution)/shard_map/pick/pallas_call | solution.py:110
  8.0 2.9 %collective-permute-start = (bf16[192,1152]{1,0:T(8,128)(2,1)S(1)}, bf16[192,1152]{1,0:T(8,128)(2,1)S(1)}, u32[]{:S(2)}, u32[]{:S(2)}) collective-permute-start(bf16[192,1152]{1,0:T(8,128)(2,1)S(1)} %pick.1), channel_id=1, source_target_pairs={{0,20},{4,16},{8,28},{12,24},{16,4},{20,0},{24,12},{28,8},{1,21},{... | collective-permute-start | bytes 1327112 | tf_op jit(solution)/shard_map/ppermute | solution.py:23
  12.2 3.3 %own.1 = (f32[8,128]{1,0:T(8,128)S(1)}, bf16[2,192,1152]{2,1,0:T(8,128)(2,1)S(1)}, bf16[2,192,1152]{2,1,0:T(8,128)(2,1)S(1)}, f32[2,192,128]{2,1,0:T(8,128)S(1)}...) custom-call(f32[1,1]{1,0:T(1,128)} %bitcast.2.exponent_ref, f32[1,1]{1,0:T(1,128)} %bitcast.3.offset_ref, ...), custom_call_target="tpu_custom_call" | custom-call | flops 1000 | bytes 1000 | tf_op jit(solution)/shard_map/own/pallas_call | solution.py:187
  15.6 0.0 collective-permute-done.1.rest_0_
  15.6 1.0 %more.2 = (f32[2,192,1152]{2,1,0:T(8,128)S(1)}, bf16[192,1152]{1,0:T(8,128)(2,1)S(1)}) custom-call(f32[8,128]{1,0:T(8,128)S(1)} %get-tuple-element.16.scale_ref, bf16[2,192,1152]{2,1,0:T(8,128)(2,1)S(1)} %get-tuple-element.17.half_ref, f32[2,192,1152]{2,1,0:T(8,128)S(1)} %get-tuple-element.19.dir_ref, ...), custom_call_target="tpu_custom_call", output_to_operand_aliasing={{0}: (2, {})} | custom-call | flops 1000 | bytes 1000 | tf_op jit(solution)/shard_map/more/pallas_call | solution.py:303
  16.6 0.1 collective-permute-start.6
  16.7 0.0 collective-permute-done.2.rest_0_
  16.7 1.3 %collective-permute-start.5 = (bf16[192,1152]{1,0:T(8,128)(2,1)S(1)}, bf16[192,1152]{1,0:T(8,128)(2,1)S(1)}, u32[]{:S(2)}, u32[]{:S(2)}) collective-permute-start(bf16[192,1152]{1,0:T(8,128)(2,1)S(1)} %get-tuple-element.26), channel_id=1, source_target_pairs={{0,4},{4,0},{8,12},{12,8},{16,20},{20,16},{24,28},{28,24},{1,5},{5... | collective-permute-start | bytes 1327112 | tf_op jit(solution)/shard_map/ppermute | solution.py:23
  18.0 4.4 %collective-permute-done.3.rest_0_ = bf16[192,1152]{1,0:T(8,128)(2,1)S(1)} collective-permute-done((bf16[192,1152]{1,0:T(8,128)(2,1)S(1)}, bf16[192,1152]{1,0:T(8,128)(2,1)S(1)}, u32[]{:S(2)}, u32[]{:S(2)}) %collective-permute-start.3) | collective-permute-done | bytes 442400 | tf_op jit(solution)/shard_map/ppermute | solution.py:23
  22.4 1.6 %collective-permute-start.7 = (bf16[192,1152]{1,0:T(8,128)(2,1)S(1)}, bf16[192,1152]{1,0:T(8,128)(2,1)S(1)}, u32[]{:S(2)}, u32[]{:S(2)}) collective-permute-start(bf16[192,1152]{1,0:T(8,128)(2,1)S(1)} %collective-permute-done.3.rest_0_), channel_id=1, source_target_pairs={{0,4},{4,0},{8,12},{12,8},{16,20},{20,16},{24,28},{28,24},{1,5},{5... | collective-permute-start | bytes 1327112 | tf_op jit(solution)/shard_map/ppermute | solution.py:23
  24.0 1.0 %more.3.dir_ref = f32[2,192,1152]{2,1,0:T(8,128)S(1)} custom-call(f32[8,128]{1,0:T(8,128)S(1)} %get-tuple-element.16.scale_ref, bf16[2,192,1152]{2,1,0:T(8,128)(2,1)S(1)} %get-tuple-element.17.half_ref, f32[2,192,1152]{2,1,0:T(8,128)S(1)} %get-tuple-element.21.dir_ref, ...), custom_call_target="tpu_custom_call", output_to_operand_aliasing={{}: (2, {})} | custom-call | flops 1000 | bytes 1000 | tf_op jit(solution)/shard_map/more/pallas_call | solution.py:303
  25.0 6.3 %collective-permute-done.raw_ref = bf16[192,1152]{1,0:T(8,128)(2,1)S(1)} collective-permute-done((bf16[192,1152]{1,0:T(8,128)(2,1)S(1)}, bf16[192,1152]{1,0:T(8,128)(2,1)S(1)}, u32[]{:S(2)}, u32[]{:S(2)}) %collective-permute-start) | collective-permute-done | bytes 442400 | tf_op jit(solution)/shard_map/ppermute | solution.py:23
  31.3 0.2 unit.1.rest_2_
  31.5 0.0 collective-permute-done.4.rest_1_
  31.5 0.0 collective-permute-done.6.rest_4_
  31.5 0.0 collective-permute-done.5.rest_3_
  31.5 2.3 %image.1 = (f32[2,192,1152]{2,1,0:T(8,128)S(1)}, f32[192,1152]{1,0:T(8,128)}) custom-call(f32[8,128]{1,0:T(8,128)S(1)} %get-tuple-element.16.scale_ref, bf16[2,192,1152]{2,1,0:T(8,128)(2,1)S(1)} %get-tuple-element.17.half_ref, f32[2,192,1152]{2,1,0:T(8,128)S(1)} %more.3.dir_ref, ...), custom_call_target="tpu_custom_call", output_to_operand_aliasing={{0}: (2, {})} | custom-call | flops 100000000 | bytes 100000000 | tf_op jit(solution)/shard_map/image/pallas_call | solution.py:335
  33.8 0.0 collective-permute-done.7.rest_0_
  33.8 1.9 %text.1 = f32[192,1152]{1,0:T(8,128)} custom-call(f32[8,128]{1,0:T(8,128)S(1)} %get-tuple-element.16.scale_ref, bf16[2,192,1152]{2,1,0:T(8,128)(2,1)S(1)} %get-tuple-element.17.half_ref, f32[2,192,1152]{2,1,0:T(8,128)S(1)} %get-tuple-element.29.dir_ref, bf16[2,192,1152]{2,1,0:T(8,128)(2,1)S(1)} %get-tuple-element.23.raw_ref, ...), custom_call_target="tpu_custom_call" | custom-call | flops 1000 | bytes 1000 | tf_op jit(solution)/shard_map/text/pallas_call | solution.py:335
Async XLA Ops:
  0.6 14.9 %collective-permute-start.1 = (bf16[192,1152]{1,0:T(8,128)(2,1)}, bf16[192,1152]{1,0:T(8,128)(2,1)S(1)}, u32[]{:S(2)}, u32[]{:S(2)}) collective-permute-start(bf16[192,1152]{1,0:T(8,128)(2,1)} %txt_ref.3), channel_id=1, source_target_pairs={{0,8},{4,12},{8,16},{12,20},{16,24},{20,28},{24,0},{28,4},{1,9},{5... | collective-permute-start | bytes 1327112 | tf_op jit(solution)/shard_map/ppermute | solution.py:23
  1.9 14.8 %collective-permute-start.2 = (bf16[192,1152]{1,0:T(8,128)(2,1)}, bf16[192,1152]{1,0:T(8,128)(2,1)S(1)}, u32[]{:S(2)}, u32[]{:S(2)}) collective-permute-start(bf16[192,1152]{1,0:T(8,128)(2,1)} %txt_ref.3), channel_id=1, source_target_pairs={{0,1},{1,2},{2,3},{3,0},{4,5},{5,6},{6,7},{7,4},{8,9},{9,10},{10,1... | collective-permute-start | bytes 1327112 | tf_op jit(solution)/shard_map/ppermute | solution.py:23
  4.6 17.8 %collective-permute-start.3 = (bf16[192,1152]{1,0:T(8,128)(2,1)S(1)}, bf16[192,1152]{1,0:T(8,128)(2,1)S(1)}, u32[]{:S(2)}, u32[]{:S(2)}) collective-permute-start(bf16[192,1152]{1,0:T(8,128)(2,1)S(1)} %norm.1.img_half), channel_id=1, source_target_pairs={{0,24},{4,28},{8,0},{12,4},{16,8},{20,12},{24,16},{28,20},{1,25},{... | collective-permute-start | bytes 1327112 | tf_op jit(solution)/shard_map/ppermute | solution.py:23
  4.9 26.6 %collective-permute-start.4 = (bf16[192,1152]{1,0:T(8,128)(2,1)S(1)}, bf16[192,1152]{1,0:T(8,128)(2,1)S(1)}, u32[]{:S(2)}, u32[]{:S(2)}) collective-permute-start(bf16[192,1152]{1,0:T(8,128)(2,1)S(1)} %norm.1.img_half), channel_id=1, source_target_pairs={{0,3},{1,0},{2,1},{3,2},{4,7},{5,4},{6,5},{7,6},{8,11},{9,8},{10,9... | collective-permute-start | bytes 1327112 | tf_op jit(solution)/shard_map/ppermute | solution.py:23
  8.0 23.3 %collective-permute-start = (bf16[192,1152]{1,0:T(8,128)(2,1)S(1)}, bf16[192,1152]{1,0:T(8,128)(2,1)S(1)}, u32[]{:S(2)}, u32[]{:S(2)}) collective-permute-start(bf16[192,1152]{1,0:T(8,128)(2,1)S(1)} %pick.1), channel_id=1, source_target_pairs={{0,20},{4,16},{8,28},{12,24},{16,4},{20,0},{24,12},{28,8},{1,21},{... | collective-permute-start | bytes 1327112 | tf_op jit(solution)/shard_map/ppermute | solution.py:23
  16.6 14.9 %collective-permute-start.6 = (bf16[192,1152]{1,0:T(8,128)(2,1)S(1)}, bf16[192,1152]{1,0:T(8,128)(2,1)S(1)}, u32[]{:S(2)}, u32[]{:S(2)}) collective-permute-start(bf16[192,1152]{1,0:T(8,128)(2,1)S(1)} %get-tuple-element.27), channel_id=1, source_target_pairs={{0,4},{4,0},{8,12},{12,8},{16,20},{20,16},{24,28},{28,24},{1,5},{5... | collective-permute-start | bytes 1327112 | tf_op jit(solution)/shard_map/ppermute | solution.py:23
  16.7 14.8 %collective-permute-start.5 = (bf16[192,1152]{1,0:T(8,128)(2,1)S(1)}, bf16[192,1152]{1,0:T(8,128)(2,1)S(1)}, u32[]{:S(2)}, u32[]{:S(2)}) collective-permute-start(bf16[192,1152]{1,0:T(8,128)(2,1)S(1)} %get-tuple-element.26), channel_id=1, source_target_pairs={{0,4},{4,0},{8,12},{12,8},{16,20},{20,16},{24,28},{28,24},{1,5},{5... | collective-permute-start | bytes 1327112 | tf_op jit(solution)/shard_map/ppermute | solution.py:23
  22.4 11.4 %collective-permute-start.7 = (bf16[192,1152]{1,0:T(8,128)(2,1)S(1)}, bf16[192,1152]{1,0:T(8,128)(2,1)S(1)}, u32[]{:S(2)}, u32[]{:S(2)}) collective-permute-start(bf16[192,1152]{1,0:T(8,128)(2,1)S(1)} %collective-permute-done.3.rest_0_), channel_id=1, source_target_pairs={{0,4},{4,0},{8,12},{12,8},{16,20},{20,16},{24,28},{28,24},{1,5},{5... | collective-permute-start | bytes 1327112 | tf_op jit(solution)/shard_map/ppermute | solution.py:23

commit v6 on v3

--- a/solution.py
+++ b/solution.py
@@ -362,6 +362,8 @@
     for d in range(2, row_extent, 2):
         text_rows.append(((0, True), along(txt, "row", lambda s: s + d)))
         image_rows.append(((1, False), along(img_half, "row", lambda s: s - d)))
+    if text_cols:
+        direction = more_visits(scale, half, direction, text_cols)
     if text_rows:
         direction, halves = more_visits(scale, half, direction, text_rows, give=True)
         per = len(halves) // len(text_rows)
@@ -370,8 +372,6 @@
             swapped.append(((0, False), [along(cut, "row", swap) for cut in block]))
     near, direction = lax.optimization_barrier((near, direction))
     swapped.append(((3, False), along(near, "row", swap)))
-    if text_cols:
-        direction = more_visits(scale, half, direction, text_cols)
     far, direction = lax.optimization_barrier((far, direction))
     middle = image_rows + image_cols + [((2, False), normalized(far))]
     middle, direction = tied(middle, direction)

time: 31.5 us -> 31.5 us (level)
  no operation moved by 1% of the time
where the time goes in v6:
time: 31.5 us; the launch traced here: 31.3 us
  starting transfers between devices  16.3 us (52%)
  Pallas kernels  12 us (38%)
  between operations  2.02 us (6%)
  waiting for transfers between devices  1.04 us (3%)
    ppermute x8, starting transfers between devices, along(): return lax.ppermute(value, axis, pairs)  16.3 us
    pallas_call x3, Pallas kernels, more_visits(): call(functools.partial(more_kernel, kinds, len(halves)), (jax.ShapeDtypeS...  3.99 us
    pallas_call x1, Pallas kernels, own_visit(): call(own_kernel, (jax.ShapeDtypeStruct((8, 128), jnp.float32), both, both...  3.31 us
    pallas_call x1, Pallas kernels, last_visits(): call(functools.partial(last_kernel, kinds), (grad, grad), [VMEM] * (5 + l...  2.01 us
    pallas_call x1, Pallas kernels, norm(): call(norm_kernel, one, [HBM], VMEM, scratch_shapes=[pltpu.VMEM(img.shape,...  1.38 us
    pallas_call x1, Pallas kernels, pick(): call(pick_kernel, jax.ShapeDtypeStruct(img.shape, img.dtype), [HBM, HBM],...  1.09 us
    ppermute x8, waiting for transfers between devices, along(): return lax.ppermute(value, axis, pairs)  1.04 us
  transfers between devices with their start and end apart: 8, of which 1 were waited for; matrix products, arithmetic and copies ran while one was open for 0% of the time, Pallas kernels for 32%

profile of v6, /device:TPU:19, one launch (start us, length us, event | category | flops | bytes accessed | tf_op | source)
XLA Modules:
  0.0 31.3 jit_solution(12103099680164321114)
XLA Ops:
  0.6 1.3 %collective-permute-start.3 = (bf16[192,1152]{1,0:T(8,128)(2,1)}, bf16[192,1152]{1,0:T(8,128)(2,1)S(1)}, u32[]{:S(2)}, u32[]{:S(2)}) collective-permute-start(bf16[192,1152]{1,0:T(8,128)(2,1)} %txt_ref.3), channel_id=1, source_target_pairs={{0,1},{1,2},{2,3},{3,0},{4,5},{5,6},{6,7},{7,4},{8,9},{9,10},{10,1... | collective-permute-start | bytes 1327112 | tf_op jit(solution)/shard_map/ppermute | solution.py:23
  2.0 1.2 %collective-permute-start.4 = (bf16[192,1152]{1,0:T(8,128)(2,1)}, bf16[192,1152]{1,0:T(8,128)(2,1)S(1)}, u32[]{:S(2)}, u32[]{:S(2)}) collective-permute-start(bf16[192,1152]{1,0:T(8,128)(2,1)} %txt_ref.3), channel_id=1, source_target_pairs={{0,8},{4,12},{8,16},{12,20},{16,24},{20,28},{24,0},{28,4},{1,9},{5... | collective-permute-start | bytes 1327112 | tf_op jit(solution)/shard_map/ppermute | solution.py:23
  3.2 1.1 %pick.1 = bf16[192,1152]{1,0:T(8,128)(2,1)S(1)} custom-call(bf16[192,1152]{1,0:T(8,128)(2,1)} %img_ref.5, bf16[192,1152]{1,0:T(8,128)(2,1)} %txt_ref.3), custom_call_target="tpu_custom_call" | custom-call | flops 1000 | bytes 1000 | tf_op jit(solution)/shard_map/pick/pallas_call | solution.py:110
  4.3 1.4 %collective-permute-start.2 = (bf16[192,1152]{1,0:T(8,128)(2,1)S(1)}, bf16[192,1152]{1,0:T(8,128)(2,1)S(1)}, u32[]{:S(2)}, u32[]{:S(2)}) collective-permute-start(bf16[192,1152]{1,0:T(8,128)(2,1)S(1)} %pick.1), channel_id=1, source_target_pairs={{0,20},{4,16},{8,28},{12,24},{16,4},{20,0},{24,12},{28,8},{1,21},{... | collective-permute-start | bytes 1327112 | tf_op jit(solution)/shard_map/ppermute | solution.py:23
  5.7 1.4 %norm.1.img_half = bf16[192,1152]{1,0:T(8,128)(2,1)S(1)} custom-call(bf16[192,1152]{1,0:T(8,128)(2,1)} %img_ref.5), custom_call_target="tpu_custom_call" | custom-call | flops 1000 | bytes 1000 | tf_op jit(solution)/shard_map/norm/pallas_call | solution.py:141
  7.1 1.3 %collective-permute-start = (bf16[192,1152]{1,0:T(8,128)(2,1)S(1)}, bf16[192,1152]{1,0:T(8,128)(2,1)S(1)}, u32[]{:S(2)}, u32[]{:S(2)}) collective-permute-start(bf16[192,1152]{1,0:T(8,128)(2,1)S(1)} %norm.1.img_half), channel_id=1, source_target_pairs={{0,24},{4,28},{8,0},{12,4},{16,8},{20,12},{24,16},{28,20},{1,25},{... | collective-permute-start | bytes 1327112 | tf_op jit(solution)/shard_map/ppermute | solution.py:23
  8.4 0.2 collective-permute-start.1
  9.9 3.3 %own.1 = (f32[8,128]{1,0:T(8,128)S(1)}, bf16[2,192,1152]{2,1,0:T(8,128)(2,1)S(1)}, bf16[2,192,1152]{2,1,0:T(8,128)(2,1)S(1)}, f32[2,192,128]{2,1,0:T(8,128)S(1)}...) custom-call(f32[1,1]{1,0:T(1,128)} %bitcast.2.exponent_ref, f32[1,1]{1,0:T(1,128)} %bitcast.3.offset_ref, ...), custom_call_target="tpu_custom_call" | custom-call | flops 1000 | bytes 1000 | tf_op jit(solution)/shard_map/own/pallas_call | solution.py:187
  13.2 0.0 collective-permute-done.3.rest_0_
  13.2 1.0 %more.3.dir_ref = f32[2,192,1152]{2,1,0:T(8,128)S(1)} custom-call(f32[8,128]{1,0:T(8,128)S(1)} %get-tuple-element.18.scale_ref, bf16[2,192,1152]{2,1,0:T(8,128)(2,1)S(1)} %get-tuple-element.19.half_ref, f32[2,192,1152]{2,1,0:T(8,128)S(1)} %get-tuple-element.21.dir_ref, ...), custom_call_target="tpu_custom_call", output_to_operand_aliasing={{}: (2, {})} | custom-call | flops 1000 | bytes 1000 | tf_op jit(solution)/shard_map/more/pallas_call | solution.py:290
  14.2 0.0 collective-permute-done.4.rest_0_
  14.2 1.0 %more.4 = (f32[2,192,1152]{2,1,0:T(8,128)S(1)}, bf16[192,1152]{1,0:T(8,128)(2,1)S(1)}) custom-call(f32[8,128]{1,0:T(8,128)S(1)} %get-tuple-element.18.scale_ref, bf16[2,192,1152]{2,1,0:T(8,128)(2,1)S(1)} %get-tuple-element.19.half_ref, f32[2,192,1152]{2,1,0:T(8,128)S(1)} %more.3.dir_ref, ...), custom_call_target="tpu_custom_call", output_to_operand_aliasing={{0}: (2, {})} | custom-call | flops 1000 | bytes 1000 | tf_op jit(solution)/shard_map/more/pallas_call | solution.py:290
  15.2 9.8 %collective-permute-start.6 = (bf16[192,1152]{1,0:T(8,128)(2,1)S(1)}, bf16[192,1152]{1,0:T(8,128)(2,1)S(1)}, u32[]{:S(2)}, u32[]{:S(2)}) collective-permute-start(bf16[192,1152]{1,0:T(8,128)(2,1)S(1)} %get-tuple-element.31), channel_id=1, source_target_pairs={{0,4},{4,0},{8,12},{12,8},{16,20},{20,16},{24,28},{28,24},{1,5},{5... | collective-permute-start | bytes 1327112 | tf_op jit(solution)/shard_map/ppermute | solution.py:23
  25.0 0.1 collective-permute-start.5
  25.1 1.0 %collective-permute-done.2.raw_ref = bf16[192,1152]{1,0:T(8,128)(2,1)S(1)} collective-permute-done((bf16[192,1152]{1,0:T(8,128)(2,1)S(1)}, bf16[192,1152]{1,0:T(8,128)(2,1)S(1)}, u32[]{:S(2)}, u32[]{:S(2)}) %collective-permute-start.2) | collective-permute-done | bytes 442400 | tf_op jit(solution)/shard_map/ppermute | solution.py:23
  26.1 0.2 unit.1.rest_2_
  26.3 0.0 collective-permute-done.rest_0_
  26.3 0.0 collective-permute-done.1.rest_1_
  26.3 0.9 %collective-permute-start.7 = (bf16[192,1152]{1,0:T(8,128)(2,1)S(1)}, bf16[192,1152]{1,0:T(8,128)(2,1)S(1)}, u32[]{:S(2)}, u32[]{:S(2)}) collective-permute-start(bf16[192,1152]{1,0:T(8,128)(2,1)S(1)} %collective-permute-done.rest_0_), channel_id=1, source_target_pairs={{0,4},{4,0},{8,12},{12,8},{16,20},{20,16},{24,28},{28,24},{1,5},{5... | collective-permute-start | bytes 1327112 | tf_op jit(solution)/shard_map/ppermute | solution.py:23
  27.3 0.0 collective-permute-done.6.rest_4_
  27.3 0.0 collective-permute-done.5.rest_3_
  27.3 2.0 %more.5.dir_ref = f32[2,192,1152]{2,1,0:T(8,128)S(1)} custom-call(f32[8,128]{1,0:T(8,128)S(1)} %get-tuple-element.18.scale_ref, bf16[2,192,1152]{2,1,0:T(8,128)(2,1)S(1)} %get-tuple-element.19.half_ref, f32[2,192,1152]{2,1,0:T(8,128)S(1)} %get-tuple-element.26.dir_ref, ...), custom_call_target="tpu_custom_call", output_to_operand_aliasing={{}: (2, {})} | custom-call | flops 4000000 | bytes 4000000 | tf_op jit(solution)/shard_map/more/pallas_call | solution.py:290
  29.3 0.0 collective-permute-done.7.rest_0_
  29.3 2.0 %last.1 = (f32[192,1152]{1,0:T(8,128)}, f32[192,1152]{1,0:T(8,128)}) custom-call(f32[8,128]{1,0:T(8,128)S(1)} %get-tuple-element.18.scale_ref, bf16[2,192,1152]{2,1,0:T(8,128)(2,1)S(1)} %get-tuple-element.19.half_ref, f32[2,192,1152]{2,1,0:T(8,128)S(1)} %more.5.dir_ref, bf16[2,192,1152]{2,1,0:T(8,128)(2,1)S(1)} %get-tuple-element.32.raw_ref, ...), custom_call_target="tpu_custom_call" | custom-call | flops 1000 | bytes 1000 | tf_op jit(solution)/shard_map/last/pallas_call | solution.py:315
Async XLA Ops:
  0.6 12.6 %collective-permute-start.3 = (bf16[192,1152]{1,0:T(8,128)(2,1)}, bf16[192,1152]{1,0:T(8,128)(2,1)S(1)}, u32[]{:S(2)}, u32[]{:S(2)}) collective-permute-start(bf16[192,1152]{1,0:T(8,128)(2,1)} %txt_ref.3), channel_id=1, source_target_pairs={{0,1},{1,2},{2,3},{3,0},{4,5},{5,6},{6,7},{7,4},{8,9},{9,10},{10,1... | collective-permute-start | bytes 1327112 | tf_op jit(solution)/shard_map/ppermute | solution.py:23
  2.0 12.2 %collective-permute-start.4 = (bf16[192,1152]{1,0:T(8,128)(2,1)}, bf16[192,1152]{1,0:T(8,128)(2,1)S(1)}, u32[]{:S(2)}, u32[]{:S(2)}) collective-permute-start(bf16[192,1152]{1,0:T(8,128)(2,1)} %txt_ref.3), channel_id=1, source_target_pairs={{0,8},{4,12},{8,16},{12,20},{16,24},{20,28},{24,0},{28,4},{1,9},{5... | collective-permute-start | bytes 1327112 | tf_op jit(solution)/shard_map/ppermute | solution.py:23
  4.3 21.8 %collective-permute-start.2 = (bf16[192,1152]{1,0:T(8,128)(2,1)S(1)}, bf16[192,1152]{1,0:T(8,128)(2,1)S(1)}, u32[]{:S(2)}, u32[]{:S(2)}) collective-permute-start(bf16[192,1152]{1,0:T(8,128)(2,1)S(1)} %pick.1), channel_id=1, source_target_pairs={{0,20},{4,16},{8,28},{12,24},{16,4},{20,0},{24,12},{28,8},{1,21},{... | collective-permute-start | bytes 1327112 | tf_op jit(solution)/shard_map/ppermute | solution.py:23
  7.1 19.2 %collective-permute-start = (bf16[192,1152]{1,0:T(8,128)(2,1)S(1)}, bf16[192,1152]{1,0:T(8,128)(2,1)S(1)}, u32[]{:S(2)}, u32[]{:S(2)}) collective-permute-start(bf16[192,1152]{1,0:T(8,128)(2,1)S(1)} %norm.1.img_half), channel_id=1, source_target_pairs={{0,24},{4,28},{8,0},{12,4},{16,8},{20,12},{24,16},{28,20},{1,25},{... | collective-permute-start | bytes 1327112 | tf_op jit(solution)/shard_map/ppermute | solution.py:23
  8.4 17.9 %collective-permute-start.1 = (bf16[192,1152]{1,0:T(8,128)(2,1)S(1)}, bf16[192,1152]{1,0:T(8,128)(2,1)S(1)}, u32[]{:S(2)}, u32[]{:S(2)}) collective-permute-start(bf16[192,1152]{1,0:T(8,128)(2,1)S(1)} %norm.1.img_half), channel_id=1, source_target_pairs={{0,3},{1,0},{2,1},{3,2},{4,7},{5,4},{6,5},{7,6},{8,11},{9,8},{10,9... | collective-permute-start | bytes 1327112 | tf_op jit(solution)/shard_map/ppermute | solution.py:23
  15.2 12.1 %collective-permute-start.6 = (bf16[192,1152]{1,0:T(8,128)(2,1)S(1)}, bf16[192,1152]{1,0:T(8,128)(2,1)S(1)}, u32[]{:S(2)}, u32[]{:S(2)}) collective-permute-start(bf16[192,1152]{1,0:T(8,128)(2,1)S(1)} %get-tuple-element.31), channel_id=1, source_target_pairs={{0,4},{4,0},{8,12},{12,8},{16,20},{20,16},{24,28},{28,24},{1,5},{5... | collective-permute-start | bytes 1327112 | tf_op jit(solution)/shard_map/ppermute | solution.py:23
  25.0 2.2 %collective-permute-start.5 = (bf16[192,1152]{1,0:T(8,128)(2,1)S(1)}, bf16[192,1152]{1,0:T(8,128)(2,1)S(1)}, u32[]{:S(2)}, u32[]{:S(2)}) collective-permute-start(bf16[192,1152]{1,0:T(8,128)(2,1)S(1)} %get-tuple-element.30), channel_id=1, source_target_pairs={{0,4},{4,0},{8,12},{12,8},{16,20},{20,16},{24,28},{28,24},{1,5},{5... | collective-permute-start | bytes 1327112 | tf_op jit(solution)/shard_map/ppermute | solution.py:23
  26.3 3.0 %collective-permute-start.7 = (bf16[192,1152]{1,0:T(8,128)(2,1)S(1)}, bf16[192,1152]{1,0:T(8,128)(2,1)S(1)}, u32[]{:S(2)}, u32[]{:S(2)}) collective-permute-start(bf16[192,1152]{1,0:T(8,128)(2,1)S(1)} %collective-permute-done.rest_0_), channel_id=1, source_target_pairs={{0,4},{4,0},{8,12},{12,8},{16,20},{20,16},{24,28},{28,24},{1,5},{5... | collective-permute-start | bytes 1327112 | tf_op jit(solution)/shard_map/ppermute | solution.py:23
